TPU v7x, 512 devices: a whole 4x4x16 slice. The times are simulated.
512 devices in a mesh: gx: 4 (over z_hi, core), gy: 32 (over z_lo, x), gz: 4 (over y).
Axes of the slice: x: 4, y: 4, z: 16 (z_hi: 2, z_lo: 8; z = z_hi * 8 + z_lo), core: 2. Of those that a mesh axis runs over, the one named last changes fastest.
Arguments:
- positions: float32 [3, 16, 32, 8, 128], P(None, 'gx', 'gy', 'gz'), as said below
- occupied: int32 [16, 32, 8, 128], P('gx', 'gy', 'gz'), may hold values 0 or 1
Outputs:
- force_out: float32 [3, 16, 32, 8, 128], P(None, 'gx', 'gy', 'gz')
- energy: float32 [16, 32, 8, 128], P('gx', 'gy', 'gz')
Inputs may be any that keep to these rules, and one draw needn't show every extreme that they name: `positions`: slot s of a tile is basis atom b = s % 4 of unit cell c = s // 4, with cell indices n_x = c // 16, n_y = (c // 4) % 4, n_z = c % 4; the basis offsets are (0, 0, 0), (0.5, 0.5, 0), (0.5, 0, 0.5), (0, 0.5, 0.5) for b = 0 to 3; each coordinate lies within 0.35 of (n + offset + 0.25) * 3.615.
All inputs are finite; a program needn't handle non-finite values. No bound on the sum of `occupied` on one device may be relied on, other than what follows from the above.
Results may differ from a plain program's by a relative error of at most 0.0003.
Values sent between devices are 32-bit elements; how exact they have to be, the bound alone decides.
A program may use at most 64 MiB of HBM per device.

v0:
```python
import jax
import jax.numpy as jnp
from jax import lax
from jax.sharding import PartitionSpec as P

SX = 2
SY = 4
SZ = 4


lattice_step = 3.615
cut_radius = 4.9
decay_rate = 5.85
bond_length = 2.556
well_depth = 0.3
morse_rate = 1.36
embed_shift = 0.5
embed_quad = 0.002


def shifted(value, axis, by):
    peers = lax.axis_size(axis)
    pairs = [(i, i + by) for i in range(peers) if 0 <= i + by < peers]
    return lax.ppermute(value, axis, pairs)


def extended(cells, sides, width):
    for axis, dim in sides:
        count = lax.axis_size(axis)
        ends = count - 1
        head = lax.slice_in_dim(cells, 0, width, axis=dim)
        tail = lax.slice_in_dim(cells, cells.shape[dim] - width, cells.shape[dim], axis=dim)
        cells = jnp.concatenate(
            [
                lax.ppermute(tail, axis, [(i, (i + 1) % count) for i in range(ends)]),
                cells,
                lax.ppermute(head, axis, [((i + 1) % count, i) for i in range(ends)]),
            ],
            axis=dim,
        )
    return cells


def pair_terms(radius_sq):
    radius = jnp.sqrt(radius_sq)
    inside = 1.0 - radius_sq / (cut_radius * cut_radius)
    smooth = inside * inside
    smooth_slope = -4.0 * radius / (cut_radius * cut_radius) * inside
    density_raw = jnp.exp(-decay_rate * (radius / bond_length - 1.0))
    density = density_raw * smooth
    density_slope = -decay_rate / bond_length * density_raw * smooth + density_raw * smooth_slope
    nearer = jnp.exp(-morse_rate * (radius - bond_length))
    bonding = well_depth * (nearer * nearer - 2.0 * nearer)
    bonding_slope = well_depth * morse_rate * (2.0 * nearer - 2.0 * nearer * nearer)
    return (
        radius,
        density,
        density_slope,
        bonding * smooth,
        bonding_slope * smooth + bonding * smooth_slope,
    )


def pair_geometry(own_tile, neighbour, offset, keep_mask):
    shift_vec = jnp.array(offset, jnp.float32).reshape((3,) + (1,) * own_tile.ndim)
    separation = neighbour[:3][..., None, :] - own_tile[:3][..., :, None] + shift_vec
    dist_sq = jnp.sum(separation * separation, axis=0)
    both_live = own_tile[3][..., :, None] * neighbour[3][..., None, :]
    within = (dist_sq < cut_radius * cut_radius) & (both_live > 0.5)
    if keep_mask is not None:
        within = within & keep_mask
    safe_sq = jnp.where(within, dist_sq, 1.0)
    return (separation, safe_sq, within.astype(jnp.float32))


def density_terms(own_tile, neighbour, offset, keep_mask):
    separation, safe_sq, weight = pair_geometry(own_tile, neighbour, offset, keep_mask)
    radius, density, density_slope, bonding, bonding_slope = pair_terms(safe_sq)
    dens_w = weight * density
    bond_w = 0.5 * weight * bonding
    own_sum = jnp.stack([jnp.sum(dens_w, -1), jnp.sum(bond_w, -1)])
    their_sum = jnp.stack([jnp.sum(dens_w, -2), jnp.sum(bond_w, -2)])
    return (own_sum, their_sum)


def force_terms(own_tile, neighbour, slope_own, slope_their, offset, keep_mask):
    separation, safe_sq, weight = pair_geometry(own_tile, neighbour, offset, keep_mask)
    radius, density, density_slope, bonding, bonding_slope = pair_terms(safe_sq)
    coupling = (
        weight
        * (bonding_slope + (slope_own[..., :, None] + slope_their[..., None, :]) * density_slope)
        / radius
    )
    pulled = separation * coupling
    return (jnp.sum(pulled, -1), -jnp.sum(pulled, -2))


def embed_terms(density):
    root_term = jnp.sqrt(density + embed_shift)
    return (
        -root_term + embed_quad * density * density,
        -0.5 / root_term + 2.0 * embed_quad * density,
    )


def half_offsets():
    upper_set = [(1, step_y, step_z) for step_y in (-1, 0, 1) for step_z in (-1, 0, 1)]
    return upper_set + [(0, 1, step_z) for step_z in (-1, 0, 1)] + [(0, 0, 1), (0, 0, 0)]


def tile_shift(step_x, step_y, step_z):
    return (step_x * SX * lattice_step, step_y * SY * lattice_step, step_z * SZ * lattice_step)


def ghosts_out(values):
    upper_layer = shifted(values[:, 0:1], "gx", -1)
    joined = jnp.concatenate([values, upper_layer], 1)
    return extended(joined, (("gy", 2), ("gz", 3)), 1)


def fold_edges(grown, axis_dim, own_count):
    inner_part = lax.slice_in_dim(grown, 2, 2 + own_count, axis=axis_dim)
    lower_edge = lax.slice_in_dim(grown, 0, 1, axis=axis_dim)
    upper_edge = lax.slice_in_dim(grown, own_count + 3, own_count + 4, axis=axis_dim)
    low_pad = [(0, 0)] * grown.ndim
    low_pad[axis_dim] = (0, own_count - 1)
    high_pad = [(0, 0)] * grown.ndim
    high_pad[axis_dim] = (own_count - 1, 0)
    return inner_part + jnp.pad(lower_edge, low_pad) + jnp.pad(upper_edge, high_pad)


def ghosts_back(totals):
    size_x = totals.shape[1] - 1
    size_y = totals.shape[2] - 2
    size_z = totals.shape[3] - 2
    grown = extended(totals, (("gy", 2), ("gz", 3)), 1)
    folded = fold_edges(fold_edges(grown, 2, size_y), 3, size_z)
    lower_layer = shifted(folded[:, size_x : size_x + 1], "gx", 1)
    own_part = folded[:, 0:size_x]
    return own_part + jnp.pad(lower_layer, ((0, 0), (0, size_x - 1), (0, 0), (0, 0), (0, 0)))


def body(positions, occupied):
    size_x, size_y, size_z, slot_count = occupied.shape
    live_f = occupied.astype(jnp.float32)
    packed = jnp.concatenate([positions, live_f[None]], 0)
    slot_row = jnp.arange(slot_count)[:, None]
    slot_col = jnp.arange(slot_count)[None, :]
    ordered = slot_row < slot_col
    grown = ghosts_out(packed)
    totals = jnp.zeros((2, size_x + 1, size_y + 2, size_z + 2, slot_count), jnp.float32)
    for step_x, step_y, step_z in half_offsets():
        neighbour = grown[
            :,
            step_x : step_x + size_x,
            1 + step_y : 1 + step_y + size_y,
            1 + step_z : 1 + step_z + size_z,
        ]
        keep_mask = ordered if (step_x, step_y, step_z) == (0, 0, 0) else None
        own_sum, their_sum = density_terms(
            packed, neighbour, tile_shift(step_x, step_y, step_z), keep_mask
        )
        totals = totals.at[:, 0:size_x, 1 : size_y + 1, 1 : size_z + 1].add(own_sum)
        totals = totals.at[
            :,
            step_x : step_x + size_x,
            1 + step_y : 1 + step_y + size_y,
            1 + step_z : 1 + step_z + size_z,
        ].add(their_sum)
    density_sums = ghosts_back(totals)
    embedding, slopes = embed_terms(density_sums[0])
    slope_grown = ghosts_out(slopes[None])
    pulls = jnp.zeros((3, size_x + 1, size_y + 2, size_z + 2, slot_count), jnp.float32)
    for step_x, step_y, step_z in half_offsets():
        neighbour = grown[
            :,
            step_x : step_x + size_x,
            1 + step_y : 1 + step_y + size_y,
            1 + step_z : 1 + step_z + size_z,
        ]
        their_slope = slope_grown[
            0,
            step_x : step_x + size_x,
            1 + step_y : 1 + step_y + size_y,
            1 + step_z : 1 + step_z + size_z,
        ]
        keep_mask = ordered if (step_x, step_y, step_z) == (0, 0, 0) else None
        own_pull, their_pull = force_terms(
            packed, neighbour, slopes, their_slope, tile_shift(step_x, step_y, step_z), keep_mask
        )
        pulls = pulls.at[:, 0:size_x, 1 : size_y + 1, 1 : size_z + 1].add(own_pull)
        pulls = pulls.at[
            :,
            step_x : step_x + size_x,
            1 + step_y : 1 + step_y + size_y,
            1 + step_z : 1 + step_z + size_z,
        ].add(their_pull)
    force_sum = ghosts_back(pulls)
    energy = live_f * (embedding + density_sums[1])
    return (force_sum * live_f[None], energy)


def solution(mesh):
    in_specs = (P(None, "gx", "gy", "gz", None), P("gx", "gy", "gz", None))
    out_specs = (P(None, "gx", "gy", "gz", None), P("gx", "gy", "gz", None))
    return jax.shard_map(body, mesh=mesh, in_specs=in_specs, out_specs=out_specs, check_vma=False)
```

profile of v0, /device:TPU:111, one launch (start us, length us, event | category | flops | bytes accessed | tf_op | source)
XLA Modules:
  0.0 188.8 jit_solution(15664316165388422304)
XLA Ops:
  2.1 2.6 %collective-permute-start = (f32[4,1,1,2,128]{4,3,2,1,0:T(2,128)S(1)}, f32[4,1,1,2,128]{4,3,2,1,0:T(2,128)S(1)}, u32[]{:S(2)}, u32[]{:S(2)}) collective-permute-start(f32[4,1,1,2,128]{4,3,2,1,0:T(2,128)S(1)} %pad_maximum_fusion.48), channel_id=1, source_target_pairs={{128,0},{256,128},{384,256},{129,1},{257,129},{385,257},{130,2},{2... | collective-permute-start | bytes 12296 | tf_op jit(solution)/shard_map/ppermute | solution.py:24
  5.4 11.3 %collective-permute-done = f32[4,1,1,2,128]{4,3,2,1,0:T(2,128)S(1)} collective-permute-done((f32[4,1,1,2,128]{4,3,2,1,0:T(2,128)S(1)}, f32[4,1,1,2,128]{4,3,2,1,0:T(2,128)S(1)}, u32[]{:S(2)}, u32[]{:S(2)}) %collective-permute-start) | collective-permute-done | bytes 4128 | tf_op jit(solution)/shard_map/ppermute | solution.py:24
  17.4 3.7 %collective-permute-start.1 = (f32[4,5,1,2,128]{4,3,2,1,0:T(2,128)S(1)}, f32[4,5,1,2,128]{4,3,2,1,0:T(2,128)S(1)}, u32[]{:S(2)}, u32[]{:S(2)}) collective-permute-start(f32[4,5,1,2,128]{4,3,2,1,0:T(2,128)S(1)} %pad_maximum_fusion.8), channel_id=1, source_target_pairs={{0,4},{4,8},{8,12},{12,16},{16,20},{20,24},{24,28},{28,32},{32,36}... | collective-permute-start | bytes 61448 | tf_op jit(solution)/shard_map/ppermute | solution.py:35
  23.1 5.9 %collective-permute-done.2 = f32[4,5,1,2,128]{4,3,2,1,0:T(2,128)S(1)} collective-permute-done((f32[4,5,1,2,128]{4,3,2,1,0:T(2,128)S(1)}, f32[4,5,1,2,128]{4,3,2,1,0:T(2,128)S(1)}, u32[]{:S(2)}, u32[]{:S(2)}) %collective-permute-start.2) | collective-permute-done | bytes 20512 | tf_op jit(solution)/shard_map/ppermute | solution.py:37
  29.8 2.1 %collective-permute-start.4 = (f32[4,5,3,1,128]{4,3,2,1,0:T(1,128)S(1)}, f32[4,5,3,1,128]{4,3,2,1,0:T(1,128)S(1)}, u32[]{:S(2)}, u32[]{:S(2)}) collective-permute-start(f32[4,5,3,1,128]{4,3,2,1,0:T(1,128)S(1)} %get-tuple-element.864), channel_id=1, source_target_pairs={{1,0},{2,1},{3,2},{5,4},{6,5},{7,6},{9,8},{10,9},{11,10},{13,12},{... | collective-permute-start | bytes 92168 | tf_op jit(solution)/shard_map/ppermute | solution.py:37
  31.9 3.2 %collective-permute-start.3 = (f32[4,5,3,1,128]{4,3,2,1,0:T(1,128)S(1)}, f32[4,5,3,1,128]{4,3,2,1,0:T(1,128)S(1)}, u32[]{:S(2)}, u32[]{:S(2)}) collective-permute-start(f32[4,5,3,1,128]{4,3,2,1,0:T(1,128)S(1)} %get-tuple-element.863), channel_id=1, source_target_pairs={{0,1},{1,2},{2,3},{4,5},{5,6},{6,7},{8,9},{9,10},{10,11},{12,13},{... | collective-permute-start | bytes 92168 | tf_op jit(solution)/shard_map/ppermute | solution.py:35
  38.1 3.3 %fusion.2 = (f32[4,2,128,128]{3,2,1,0:T(8,128)S(1)}, f32[4,2,128,128]{3,2,1,0:T(8,128)S(1)}, f32[4,2,128,128]{3,2,1,0:T(8,128)S(1)}, f32[4,2,128,128]{3,2,1,0:T(...) fusion(f32[3,4,2,128]{3,2,1,0:T(2,128)S(1)} %bitcast.234, ...), kind=kLoop, calls=%fused_computation.4 | loop fusion | flops 14024704 | bytes 5365868 | tf_op jit(solution)/shard_map/reduce_sum | solution.py:67
  41.5 4.7 %fusion.181 = (f32[4,2,128]{2,1,0:T(2,128)}, f32[4,2,128]{2,1,0:T(2,128)}, f32[4,2,128]{2,1,0:T(2,128)}, f32[4,2,128]{2,1,0:T(2,128)}, f32[4,2,128]{2,1,0:T(2,12...) fusion(f32[4,2,128,128]{3,2,1,0:T(8,128)S(1)} %get-tuple-elemen, ...), kind=kLoop, calls=%fused_computation.330 | loop fusion | flops 15718400 | bytes 5308416 | tf_op jit(solution)/shard_map/reduce_sum | solution.py:82
  46.7 7.1 %fusion.199 = (f32[4,2,128]{2,1,0:T(2,128)S(1)}, f32[4,2,128]{2,1,0:T(2,128)S(1)}, f32[4,2,128]{2,1,0:T(2,128)S(1)}, f32[4,2,128]{2,1,0:T(2,128)S(1)}, f32[4,2,1...) fusion(f32[4,2,128,128]{3,2,1,0:T(8,128)S(1)} %get-tuple-elemen, ...), kind=kLoop, calls=%fused_computation.355 | loop fusion | flops 28424192 | bytes 9564160 | tf_op jit(solution)/shard_map/reduce_sum | solution.py:82
  56.5 2.1 %fusion.247 = (f32[4,2,128]{2,1,0:T(2,128)S(1)}, f32[4,2,128]{2,1,0:T(2,128)S(1)}, f32[4,2,128]{2,1,0:T(2,128)S(1)}, f32[4,2,128]{2,1,0:T(2,128)}) fusion(f32[4,2,128,128]{3,2,1,0:T(8,128)} %get-tuple-element.833, f32[4,2,128,128]{3,2,1,0:T(8,128)} %get-tuple-element.834), kind=kLoop, calls=%fused_computation.543 | loop fusion | flops 520192 | bytes 1064960 | tf_op jit(solution)/shard_map/reduce_sum | solution.py:82
  71.3 2.1 %scatter-add.229 = f32[2,5,3,4,128]{4,3,1,2,0:T(4,128)S(1)} dynamic-update-slice(f32[2,5,3,4,128]{4,3,1,2,0:T(4,128)S(1)} %scatter-add.226, f32[2,4,1,2,128]{4,3,1,2,0:T(2,128)S(1)} %maximum_add_fusion, s32[]{:T(128)} %constant.1581.clone.1, s32[]{:T(128)} %bitcast.81, s32[]{:T(128)} %bitcast.82, s32[]{:T(128)} %bitcast.83, s32[]{:T(128)} %constant.1581.clone.1) | dynamic-update-slice | bytes 16388 | tf_op jit(solution)/shard_map/scatter-add | solution.py:169
  75.8 3.5 %collective-permute-start.6 = (f32[2,5,1,4,128]{4,3,1,2,0:T(4,128)S(1)}, f32[2,5,1,4,128]{4,3,1,2,0:T(4,128)S(1)}, u32[]{:S(2)}, u32[]{:S(2)}) collective-permute-start(f32[2,5,1,4,128]{4,3,1,2,0:T(4,128)S(1)} %get-tuple-element.859), channel_id=1, source_target_pairs={{4,0},{8,4},{12,8},{16,12},{20,16},{24,20},{28,24},{32,28},{36,32}... | collective-permute-start | bytes 61448 | tf_op jit(solution)/shard_map/ppermute | solution.py:37
  79.4 4.3 %collective-permute-done.6 = f32[2,5,1,4,128]{4,3,1,2,0:T(4,128)S(1)} collective-permute-done((f32[2,5,1,4,128]{4,3,1,2,0:T(4,128)S(1)}, f32[2,5,1,4,128]{4,3,1,2,0:T(4,128)S(1)}, u32[]{:S(2)}, u32[]{:S(2)}) %collective-permute-start.6) | collective-permute-done | bytes 20512 | tf_op jit(solution)/shard_map/ppermute | solution.py:37
  83.7 3.2 %collective-permute-start.7 = (f32[2,5,5,1,128]{4,3,1,2,0:T(1,128)S(1)}, f32[2,5,5,1,128]{4,3,1,2,0:T(1,128)S(1)}, u32[]{:S(2)}, u32[]{:S(2)}) collective-permute-start(f32[2,5,5,1,128]{4,3,1,2,0:T(1,128)S(1)} %get-tuple-element.840), channel_id=1, source_target_pairs={{0,1},{1,2},{2,3},{4,5},{5,6},{6,7},{8,9},{9,10},{10,11},{12,13},{... | collective-permute-start | bytes 76808 | tf_op jit(solution)/shard_map/ppermute | solution.py:35
  86.9 2.1 %collective-permute-start.8 = (f32[2,5,5,1,128]{4,3,1,2,0:T(1,128)S(1)}, f32[2,5,5,1,128]{4,3,1,2,0:T(1,128)S(1)}, u32[]{:S(2)}, u32[]{:S(2)}) collective-permute-start(f32[2,5,5,1,128]{4,3,1,2,0:T(1,128)S(1)} %get-tuple-element.841), channel_id=1, source_target_pairs={{1,0},{2,1},{3,2},{5,4},{6,5},{7,6},{9,8},{10,9},{11,10},{13,12},{... | collective-permute-start | bytes 76808 | tf_op jit(solution)/shard_map/ppermute | solution.py:37
  89.0 2.5 %collective-permute-done.8 = f32[2,5,5,1,128]{4,3,1,2,0:T(1,128)S(1)} collective-permute-done((f32[2,5,5,1,128]{4,3,1,2,0:T(1,128)S(1)}, f32[2,5,5,1,128]{4,3,1,2,0:T(1,128)S(1)}, u32[]{:S(2)}, u32[]{:S(2)}) %collective-permute-start.8) | collective-permute-done | bytes 25632 | tf_op jit(solution)/shard_map/ppermute | solution.py:37
  91.7 7.4 %collective-permute-start.9 = (f32[2,1,1,2,128]{4,3,1,2,0:T(2,128)S(1)}, f32[2,1,1,2,128]{4,3,1,2,0:T(2,128)S(1)}, u32[]{:S(2)}, u32[]{:S(2)}) collective-permute-start(f32[2,1,1,2,128]{4,3,1,2,0:T(2,128)S(1)} %slice.2773), channel_id=1, source_target_pairs={{0,128},{128,256},{256,384},{1,129},{129,257},{257,385},{2,130},{1... | collective-permute-start | bytes 6152 | tf_op jit(solution)/shard_map/ppermute | solution.py:24
  101.7 12.2 %collective-permute-done.10 = f32[1,1,1,2,128]{4,3,1,2,0:T(2,128)S(1)} collective-permute-done((f32[1,1,1,2,128]{4,3,1,2,0:T(2,128)S(1)}, f32[1,1,1,2,128]{4,3,1,2,0:T(2,128)S(1)}, u32[]{:S(2)}, u32[]{:S(2)}) %collective-permute-start.10) | collective-permute-done | bytes 1056 | tf_op jit(solution)/shard_map/ppermute | solution.py:24
  115.9 3.4 %collective-permute-start.12 = (f32[1,5,1,2,128]{4,3,1,2,0:T(2,128)S(1)}, f32[1,5,1,2,128]{4,3,1,2,0:T(2,128)S(1)}, u32[]{:S(2)}, u32[]{:S(2)}) collective-permute-start(f32[1,5,1,2,128]{4,3,1,2,0:T(2,128)S(1)} %pad_maximum_fusion.22), channel_id=1, source_target_pairs={{4,0},{8,4},{12,8},{16,12},{20,16},{24,20},{28,24},{32,28},{36,32}... | collective-permute-start | bytes 15368 | tf_op jit(solution)/shard_map/ppermute | solution.py:37
  119.3 4.3 %collective-permute-done.12 = f32[1,5,1,2,128]{4,3,1,2,0:T(2,128)S(1)} collective-permute-done((f32[1,5,1,2,128]{4,3,1,2,0:T(2,128)S(1)}, f32[1,5,1,2,128]{4,3,1,2,0:T(2,128)S(1)}, u32[]{:S(2)}, u32[]{:S(2)}) %collective-permute-start.12) | collective-permute-done | bytes 5152 | tf_op jit(solution)/shard_map/ppermute | solution.py:37
  125.7 3.2 %collective-permute-start.13 = (f32[1,5,3,1,128]{4,3,1,2,0:T(1,128)S(1)}, f32[1,5,3,1,128]{4,3,1,2,0:T(1,128)S(1)}, u32[]{:S(2)}, u32[]{:S(2)}) collective-permute-start(f32[1,5,3,1,128]{4,3,1,2,0:T(1,128)S(1)} %get-tuple-element.881), channel_id=1, source_target_pairs={{0,1},{1,2},{2,3},{4,5},{5,6},{6,7},{8,9},{9,10},{10,11},{12,13},{... | collective-permute-start | bytes 23048 | tf_op jit(solution)/shard_map/ppermute | solution.py:35
  130.2 3.3 %fusion.127 = (f32[4,2,128,128]{3,2,1,0:T(8,128)}, f32[4,2,128,128]{3,2,1,0:T(8,128)}, f32[4,2,128,128]{3,2,1,0:T(8,128)S(1)}) fusion(f32[4,2,128,128]{3,2,1,0:T(8,128)S(1)} %get-tuple-element.794, f32[4,2,128]{2,1,0:T(2,128)S(1)} %get-tuple-element.866, f32[4,2,128]{2,1,0:T(2,128)S(1)} %fusion.257, f32[4,2,128]{2,1,0:T(2,128)S(1)} %get-tuple-element.849, ...), kind=kLoop, calls=%fused_computation.183 | loop fusion | flops 13369344 | bytes 3178496 | tf_op jit(solution)/shard_map/div | solution.py:90
  133.6 5.8 %fusion.109 = (f32[4,2,128,128]{3,2,1,0:T(8,128)S(1)}, f32[4,2,128,128]{3,2,1,0:T(8,128)S(1)}, f32[4,2,128,128]{3,2,1,0:T(8,128)}, f32[4,2,128,128]{3,2,1,0:T(8,...) fusion(f32[4,2,128,128]{3,2,1,0:T(8,128)S(1)} %copy-done.5, f32[4,2,128]{2,1,0:T(2,128)S(1)} %get-tuple-element.865, ...), kind=kLoop, calls=%fused_computation.165 | loop fusion | flops 26869760 | bytes 6356992 | tf_op jit(solution)/shard_map/div | solution.py:90
  141.6 4.9 %fusion.115 = (f32[4,2,128,128]{3,2,1,0:T(8,128)}, f32[4,2,128,128]{3,2,1,0:T(8,128)S(1)}, f32[4,2,128,128]{3,2,1,0:T(8,128)S(1)}, f32[4,2,128,128]{3,2,1,0:T(8,128)S(1)}, f32[4,2,128,128]{3,2,1,0:T(8,128)}) fusion(f32[4,2,128,128]{3,2,1,0:T(8,128)S(1)} %copy-done.1, f32[4,2,128]{2,1,0:T(2,128)S(1)} %get-tuple-element.868, f32[4,2,128]{2,1,0:T(2,128)S(1)} %fusion.257, ...), kind=kLoop, calls=%fused_computation.171 | loop fusion | flops 22282240 | bytes 5292032 | tf_op jit(solution)/shard_map/div | solution.py:90
  146.6 3.7 %fusion.19 = (f32[3,4,2,128]{3,2,1,0:T(2,128)S(1)}, f32[3,4,2,128]{3,2,1,0:T(2,128)S(1)}, f32[3,4,2,128]{3,2,1,0:T(2,128)S(1)}, f32[3,4,2,128]{3,2,1,0:T(2,128)S...) fusion(f32[4,2,128,128]{3,2,1,0:T(8,128)S(1)} %get-tuple-elemen, ...), kind=kLoop, calls=%fused_computation.33 | loop fusion | flops 11759616 | bytes 3379272 | tf_op jit(solution)/shard_map/reduce_sum | solution.py:95
  152.1 4.4 %fusion = (f32[3,4,2,128]{3,2,1,0:T(2,128)S(1)}, f32[3,4,2,128]{3,2,1,0:T(2,128)S(1)}, f32[3,4,2,128]{3,2,1,0:T(2,128)S(1)}, f32[3,4,2,128]{3,2,1,0:T(2,128)S(1)...) fusion(f32[4,2,128,128]{3,2,1,0:T(8,128)S(1)} %copy-done.19, ...), kind=kLoop, calls=%fused_computation.2 | loop fusion | flops 11366400 | bytes 3366972 | tf_op jit(solution)/shard_map/reduce_sum | solution.py:95
  159.7 2.1 %scatter-add.275 = f32[3,5,3,4,128]{4,3,1,0,2:T(4,128)S(1)} dynamic-update-slice(f32[3,5,3,4,128]{4,3,1,0,2:T(4,128)S(1)} %scatter-add.274, f32[3,4,1,2,128]{4,3,1,0,2:T(2,128)S(1)} %bitcast_add_fusion.1, s32[]{:T(128)} %constant.1581.clone.1, s32[]{:T(128)} %bitcast.81, s32[]{:T(128)} %bitcast.82, s32[]{:T(128)} %bitcast.83, s32[]{:T(128)} %constant.1581.clone.1) | dynamic-update-slice | bytes 24580 | tf_op jit(solution)/shard_map/scatter-add | solution.py:197
  164.2 3.4 %collective-permute-start.16 = (f32[3,5,1,4,128]{4,3,1,0,2:T(4,128)S(1)}, f32[3,5,1,4,128]{4,3,1,0,2:T(4,128)S(1)}, u32[]{:S(2)}, u32[]{:S(2)}) collective-permute-start(f32[3,5,1,4,128]{4,3,1,0,2:T(4,128)S(1)} %get-tuple-element.843), channel_id=1, source_target_pairs={{4,0},{8,4},{12,8},{16,12},{20,16},{24,20},{28,24},{32,28},{36,32}... | collective-permute-start | bytes 92168 | tf_op jit(solution)/shard_map/ppermute | solution.py:37
  167.5 4.6 %collective-permute-done.16 = f32[3,5,1,4,128]{4,3,1,0,2:T(4,128)S(1)} collective-permute-done((f32[3,5,1,4,128]{4,3,1,0,2:T(4,128)S(1)}, f32[3,5,1,4,128]{4,3,1,0,2:T(4,128)S(1)}, u32[]{:S(2)}, u32[]{:S(2)}) %collective-permute-start.16) | collective-permute-done | bytes 30752 | tf_op jit(solution)/shard_map/ppermute | solution.py:37
  172.2 3.2 %collective-permute-start.17 = (f32[3,5,5,1,128]{4,3,1,0,2:T(1,128)S(1)}, f32[3,5,5,1,128]{4,3,1,0,2:T(1,128)S(1)}, u32[]{:S(2)}, u32[]{:S(2)}) collective-permute-start(f32[3,5,5,1,128]{4,3,1,0,2:T(1,128)S(1)} %get-tuple-element.838), channel_id=1, source_target_pairs={{0,1},{1,2},{2,3},{4,5},{5,6},{6,7},{8,9},{9,10},{10,11},{12,13},{... | collective-permute-start | bytes 115208 | tf_op jit(solution)/shard_map/ppermute | solution.py:35
  177.5 2.6 %collective-permute-done.18 = f32[3,5,5,1,128]{4,3,1,0,2:T(1,128)S(1)} collective-permute-done((f32[3,5,5,1,128]{4,3,1,0,2:T(1,128)S(1)}, f32[3,5,5,1,128]{4,3,1,0,2:T(1,128)S(1)}, u32[]{:S(2)}, u32[]{:S(2)}) %collective-permute-start.18) | collective-permute-done | bytes 38432 | tf_op jit(solution)/shard_map/ppermute | solution.py:37
  180.3 7.1 %collective-permute-start.19 = (f32[3,1,1,2,128]{4,3,1,0,2:T(2,128)S(1)}, f32[3,1,1,2,128]{4,3,1,0,2:T(2,128)S(1)}, u32[]{:S(2)}, u32[]{:S(2)}) collective-permute-start(f32[3,1,1,2,128]{4,3,1,0,2:T(2,128)S(1)} %slice.2810), channel_id=1, source_target_pairs={{0,128},{128,256},{256,384},{1,129},{129,257},{257,385},{2,130},{1... | collective-permute-start | bytes 9224 | tf_op jit(solution)/shard_map/ppermute | solution.py:24
  (267 shorter events, 46.9 us)
Async XLA Ops:
  0.6 35.9 %copy-start.39 = (f32[3]{0:T(128)S(1)}, f32[3]{0:T(128)}, u32[]{:S(2)}) copy-start(f32[3]{0:T(128)} %constant.1588.clone) | copy-start | bytes 40
  0.6 35.9 %copy-start.30 = (f32[3]{0:T(128)S(1)}, f32[3]{0:T(128)}, u32[]{:S(2)}) copy-start(f32[3]{0:T(128)} %constant.1598.clone) | copy-start | bytes 40
  0.7 35.9 %copy-start.32 = (f32[3]{0:T(128)S(1)}, f32[3]{0:T(128)}, u32[]{:S(2)}) copy-start(f32[3]{0:T(128)} %constant.1599.clone) | copy-start | bytes 40
  0.7 35.9 %copy-start.34 = (f32[3]{0:T(128)S(1)}, f32[3]{0:T(128)}, u32[]{:S(2)}) copy-start(f32[3]{0:T(128)} %constant.1600.clone) | copy-start | bytes 40
  0.7 35.2 %copy-start.16 = (f32[3,4,1,2,128]{4,3,2,1,0:T(2,128)S(1)}, f32[3,4,1,2,128]{4,3,2,1,0:T(2,128)}, u32[]{:S(2)}) copy-start(f32[3,4,1,2,128]{4,3,2,1,0:T(2,128)} %param.142) | copy-start | bytes 36868
  2.1 14.6 %collective-permute-start = (f32[4,1,1,2,128]{4,3,2,1,0:T(2,128)S(1)}, f32[4,1,1,2,128]{4,3,2,1,0:T(2,128)S(1)}, u32[]{:S(2)}, u32[]{:S(2)}) collective-permute-start(f32[4,1,1,2,128]{4,3,2,1,0:T(2,128)S(1)} %pad_maximum_fusion.48), channel_id=1, source_target_pairs={{128,0},{256,128},{384,256},{129,1},{257,129},{385,257},{130,2},{2... | collective-permute-start | bytes 12296 | tf_op jit(solution)/shard_map/ppermute | solution.py:24
  17.4 5.7 %collective-permute-start.1 = (f32[4,5,1,2,128]{4,3,2,1,0:T(2,128)S(1)}, f32[4,5,1,2,128]{4,3,2,1,0:T(2,128)S(1)}, u32[]{:S(2)}, u32[]{:S(2)}) collective-permute-start(f32[4,5,1,2,128]{4,3,2,1,0:T(2,128)S(1)} %pad_maximum_fusion.8), channel_id=1, source_target_pairs={{0,4},{4,8},{8,12},{12,16},{16,20},{20,24},{24,28},{28,32},{32,36}... | collective-permute-start | bytes 61448 | tf_op jit(solution)/shard_map/ppermute | solution.py:35
  21.1 7.8 %collective-permute-start.2 = (f32[4,5,1,2,128]{4,3,2,1,0:T(2,128)S(1)}, f32[4,5,1,2,128]{4,3,2,1,0:T(2,128)S(1)}, u32[]{:S(2)}, u32[]{:S(2)}) collective-permute-start(f32[4,5,1,2,128]{4,3,2,1,0:T(2,128)S(1)} %pad_maximum_fusion.8), channel_id=1, source_target_pairs={{4,0},{8,4},{12,8},{16,12},{20,16},{24,20},{28,24},{32,28},{36,32}... | collective-permute-start | bytes 61448 | tf_op jit(solution)/shard_map/ppermute | solution.py:37
  29.8 5.3 %collective-permute-start.4 = (f32[4,5,3,1,128]{4,3,2,1,0:T(1,128)S(1)}, f32[4,5,3,1,128]{4,3,2,1,0:T(1,128)S(1)}, u32[]{:S(2)}, u32[]{:S(2)}) collective-permute-start(f32[4,5,3,1,128]{4,3,2,1,0:T(1,128)S(1)} %get-tuple-element.864), channel_id=1, source_target_pairs={{1,0},{2,1},{3,2},{5,4},{6,5},{7,6},{9,8},{10,9},{11,10},{13,12},{... | collective-permute-start | bytes 92168 | tf_op jit(solution)/shard_map/ppermute | solution.py:37
  31.9 4.6 %collective-permute-start.3 = (f32[4,5,3,1,128]{4,3,2,1,0:T(1,128)S(1)}, f32[4,5,3,1,128]{4,3,2,1,0:T(1,128)S(1)}, u32[]{:S(2)}, u32[]{:S(2)}) collective-permute-start(f32[4,5,3,1,128]{4,3,2,1,0:T(1,128)S(1)} %get-tuple-element.863), channel_id=1, source_target_pairs={{0,1},{1,2},{2,3},{4,5},{5,6},{6,7},{8,9},{9,10},{10,11},{12,13},{... | collective-permute-start | bytes 92168 | tf_op jit(solution)/shard_map/ppermute | solution.py:35
  69.2 22.4 %copy-start.29 = (pred[2]{0:T(512)(128)(4,1)S(1)}, pred[2]{0:T(512)(128)(4,1)}, u32[]{:S(2)}) copy-start(pred[2]{0:T(512)(128)(4,1)} %constant.1584.clone.1) | copy-start | bytes 10
  73.7 56.4 %copy-start.7 = (f32[4,2,128,128]{3,2,1,0:T(8,128)S(1)}, f32[4,2,128,128]{3,2,1,0:T(8,128)}, u32[]{:S(2)}) copy-start(f32[4,2,128,128]{3,2,1,0:T(8,128)} %copy-done.6) | copy-start | bytes 1572868
  73.8 5.6 %collective-permute-start.5 = (f32[2,5,1,4,128]{4,3,1,2,0:T(4,128)S(1)}, f32[2,5,1,4,128]{4,3,1,2,0:T(4,128)S(1)}, u32[]{:S(2)}, u32[]{:S(2)}) collective-permute-start(f32[2,5,1,4,128]{4,3,1,2,0:T(4,128)S(1)} %get-tuple-element.858), channel_id=1, source_target_pairs={{0,4},{4,8},{8,12},{12,16},{16,20},{20,24},{24,28},{28,32},{32,36}... | collective-permute-start | bytes 61448 | tf_op jit(solution)/shard_map/ppermute | solution.py:35
  75.8 7.8 %collective-permute-start.6 = (f32[2,5,1,4,128]{4,3,1,2,0:T(4,128)S(1)}, f32[2,5,1,4,128]{4,3,1,2,0:T(4,128)S(1)}, u32[]{:S(2)}, u32[]{:S(2)}) collective-permute-start(f32[2,5,1,4,128]{4,3,1,2,0:T(4,128)S(1)} %get-tuple-element.859), channel_id=1, source_target_pairs={{4,0},{8,4},{12,8},{16,12},{20,16},{24,20},{28,24},{32,28},{36,32}... | collective-permute-start | bytes 61448 | tf_op jit(solution)/shard_map/ppermute | solution.py:37
  83.7 5.3 %collective-permute-start.7 = (f32[2,5,5,1,128]{4,3,1,2,0:T(1,128)S(1)}, f32[2,5,5,1,128]{4,3,1,2,0:T(1,128)S(1)}, u32[]{:S(2)}, u32[]{:S(2)}) collective-permute-start(f32[2,5,5,1,128]{4,3,1,2,0:T(1,128)S(1)} %get-tuple-element.840), channel_id=1, source_target_pairs={{0,1},{1,2},{2,3},{4,5},{5,6},{6,7},{8,9},{9,10},{10,11},{12,13},{... | collective-permute-start | bytes 76808 | tf_op jit(solution)/shard_map/ppermute | solution.py:35
  86.9 4.6 %collective-permute-start.8 = (f32[2,5,5,1,128]{4,3,1,2,0:T(1,128)S(1)}, f32[2,5,5,1,128]{4,3,1,2,0:T(1,128)S(1)}, u32[]{:S(2)}, u32[]{:S(2)}) collective-permute-start(f32[2,5,5,1,128]{4,3,1,2,0:T(1,128)S(1)} %get-tuple-element.841), channel_id=1, source_target_pairs={{1,0},{2,1},{3,2},{5,4},{6,5},{7,6},{9,8},{10,9},{11,10},{13,12},{... | collective-permute-start | bytes 76808 | tf_op jit(solution)/shard_map/ppermute | solution.py:37
  91.7 8.1 %collective-permute-start.9 = (f32[2,1,1,2,128]{4,3,1,2,0:T(2,128)S(1)}, f32[2,1,1,2,128]{4,3,1,2,0:T(2,128)S(1)}, u32[]{:S(2)}, u32[]{:S(2)}) collective-permute-start(f32[2,1,1,2,128]{4,3,1,2,0:T(2,128)S(1)} %slice.2773), channel_id=1, source_target_pairs={{0,128},{128,256},{256,384},{1,129},{129,257},{257,385},{2,130},{1... | collective-permute-start | bytes 6152 | tf_op jit(solution)/shard_map/ppermute | solution.py:24
  99.8 14.1 %collective-permute-start.10 = (f32[1,1,1,2,128]{4,3,1,2,0:T(2,128)S(1)}, f32[1,1,1,2,128]{4,3,1,2,0:T(2,128)S(1)}, u32[]{:S(2)}, u32[]{:S(2)}) collective-permute-start(f32[1,1,1,2,128]{4,3,1,2,0:T(2,128)S(1)} %slice.2775), channel_id=1, source_target_pairs={{128,0},{256,128},{384,256},{129,1},{257,129},{385,257},{130,2},{2... | collective-permute-start | bytes 3080 | tf_op jit(solution)/shard_map/ppermute | solution.py:24
  114.0 5.3 %collective-permute-start.11 = (f32[1,5,1,2,128]{4,3,1,2,0:T(2,128)S(1)}, f32[1,5,1,2,128]{4,3,1,2,0:T(2,128)S(1)}, u32[]{:S(2)}, u32[]{:S(2)}) collective-permute-start(f32[1,5,1,2,128]{4,3,1,2,0:T(2,128)S(1)} %pad_maximum_fusion.22), channel_id=1, source_target_pairs={{0,4},{4,8},{8,12},{12,16},{16,20},{20,24},{24,28},{28,32},{32,36}... | collective-permute-start | bytes 15368 | tf_op jit(solution)/shard_map/ppermute | solution.py:35
  115.9 7.7 %collective-permute-start.12 = (f32[1,5,1,2,128]{4,3,1,2,0:T(2,128)S(1)}, f32[1,5,1,2,128]{4,3,1,2,0:T(2,128)S(1)}, u32[]{:S(2)}, u32[]{:S(2)}) collective-permute-start(f32[1,5,1,2,128]{4,3,1,2,0:T(2,128)S(1)} %pad_maximum_fusion.22), channel_id=1, source_target_pairs={{4,0},{8,4},{12,8},{16,12},{20,16},{24,20},{28,24},{32,28},{36,32}... | collective-permute-start | bytes 15368 | tf_op jit(solution)/shard_map/ppermute | solution.py:37
  123.6 5.3 %collective-permute-start.14 = (f32[1,5,3,1,128]{4,3,1,2,0:T(1,128)S(1)}, f32[1,5,3,1,128]{4,3,1,2,0:T(1,128)S(1)}, u32[]{:S(2)}, u32[]{:S(2)}) collective-permute-start(f32[1,5,3,1,128]{4,3,1,2,0:T(1,128)S(1)} %get-tuple-element.880), channel_id=1, source_target_pairs={{1,0},{2,1},{3,2},{5,4},{6,5},{7,6},{9,8},{10,9},{11,10},{13,12},{... | collective-permute-start | bytes 23048 | tf_op jit(solution)/shard_map/ppermute | solution.py:37
  125.7 4.4 %collective-permute-start.13 = (f32[1,5,3,1,128]{4,3,1,2,0:T(1,128)S(1)}, f32[1,5,3,1,128]{4,3,1,2,0:T(1,128)S(1)}, u32[]{:S(2)}, u32[]{:S(2)}) collective-permute-start(f32[1,5,3,1,128]{4,3,1,2,0:T(1,128)S(1)} %get-tuple-element.881), channel_id=1, source_target_pairs={{0,1},{1,2},{2,3},{4,5},{5,6},{6,7},{8,9},{9,10},{10,11},{12,13},{... | collective-permute-start | bytes 23048 | tf_op jit(solution)/shard_map/ppermute | solution.py:35
  133.6 5.9 %copy-start.40 = (f32[3]{0:T(128)S(1)}, f32[3]{0:T(128)}, u32[]{:S(2)}) copy-start(f32[3]{0:T(128)} %constant.1588.clone) | copy-start | bytes 40
  133.6 5.9 %copy-start.42 = (f32[3]{0:T(128)S(1)}, f32[3]{0:T(128)}, u32[]{:S(2)}) copy-start(f32[3]{0:T(128)} %constant.1589.clone) | copy-start | bytes 40
  146.6 5.5 %copy-start.18 = (f32[4,2,128,128]{3,2,1,0:T(8,128)S(1)}, f32[4,2,128,128]{3,2,1,0:T(8,128)}, u32[]{:S(2)}) copy-start(f32[4,2,128,128]{3,2,1,0:T(8,128)} %get-tuple-element.894) | copy-start | bytes 1572868
  146.6 5.5 %copy-start.19 = (f32[4,2,128,128]{3,2,1,0:T(8,128)S(1)}, f32[4,2,128,128]{3,2,1,0:T(8,128)}, u32[]{:S(2)}) copy-start(f32[4,2,128,128]{3,2,1,0:T(8,128)} %get-tuple-element.887) | copy-start | bytes 1572868
  157.8 29.7 %copy-start.26 = (s32[4,1,2,128]{3,2,1,0:T(2,128)S(1)}, s32[4,1,2,128]{3,2,1,0:T(2,128)}, u32[]{:S(2)}) copy-start(s32[4,1,2,128]{3,2,1,0:T(2,128)} %param.143) | copy-start | bytes 12292
  162.2 5.3 %collective-permute-start.15 = (f32[3,5,1,4,128]{4,3,1,0,2:T(4,128)S(1)}, f32[3,5,1,4,128]{4,3,1,0,2:T(4,128)S(1)}, u32[]{:S(2)}, u32[]{:S(2)}) collective-permute-start(f32[3,5,1,4,128]{4,3,1,0,2:T(4,128)S(1)} %get-tuple-element.842), channel_id=1, source_target_pairs={{0,4},{4,8},{8,12},{12,16},{16,20},{20,24},{24,28},{28,32},{32,36}... | collective-permute-start | bytes 92168 | tf_op jit(solution)/shard_map/ppermute | solution.py:35
  164.2 8.0 %collective-permute-start.16 = (f32[3,5,1,4,128]{4,3,1,0,2:T(4,128)S(1)}, f32[3,5,1,4,128]{4,3,1,0,2:T(4,128)S(1)}, u32[]{:S(2)}, u32[]{:S(2)}) collective-permute-start(f32[3,5,1,4,128]{4,3,1,0,2:T(4,128)S(1)} %get-tuple-element.843), channel_id=1, source_target_pairs={{4,0},{8,4},{12,8},{16,12},{20,16},{24,20},{28,24},{32,28},{36,32}... | collective-permute-start | bytes 92168 | tf_op jit(solution)/shard_map/ppermute | solution.py:37
  172.2 5.3 %collective-permute-start.17 = (f32[3,5,5,1,128]{4,3,1,0,2:T(1,128)S(1)}, f32[3,5,5,1,128]{4,3,1,0,2:T(1,128)S(1)}, u32[]{:S(2)}, u32[]{:S(2)}) collective-permute-start(f32[3,5,5,1,128]{4,3,1,0,2:T(1,128)S(1)} %get-tuple-element.838), channel_id=1, source_target_pairs={{0,1},{1,2},{2,3},{4,5},{5,6},{6,7},{8,9},{9,10},{10,11},{12,13},{... | collective-permute-start | bytes 115208 | tf_op jit(solution)/shard_map/ppermute | solution.py:35
  175.4 4.7 %collective-permute-start.18 = (f32[3,5,5,1,128]{4,3,1,0,2:T(1,128)S(1)}, f32[3,5,5,1,128]{4,3,1,0,2:T(1,128)S(1)}, u32[]{:S(2)}, u32[]{:S(2)}) collective-permute-start(f32[3,5,5,1,128]{4,3,1,0,2:T(1,128)S(1)} %get-tuple-element.839), channel_id=1, source_target_pairs={{1,0},{2,1},{3,2},{5,4},{6,5},{7,6},{9,8},{10,9},{11,10},{13,12},{... | collective-permute-start | bytes 115208 | tf_op jit(solution)/shard_map/ppermute | solution.py:37
  180.3 7.8 %collective-permute-start.19 = (f32[3,1,1,2,128]{4,3,1,0,2:T(2,128)S(1)}, f32[3,1,1,2,128]{4,3,1,0,2:T(2,128)S(1)}, u32[]{:S(2)}, u32[]{:S(2)}) collective-permute-start(f32[3,1,1,2,128]{4,3,1,0,2:T(2,128)S(1)} %slice.2810), channel_id=1, source_target_pairs={{0,128},{128,256},{256,384},{1,129},{129,257},{257,385},{2,130},{1... | collective-permute-start | bytes 9224 | tf_op jit(solution)/shard_map/ppermute | solution.py:24
  (43 other events, 147.7 us)
where the time goes:
time: 190 us; the launch traced here: 189 us
  other arithmetic  63.3 us (33%)
  starting transfers between devices  61.9 us (33%)
  waiting for transfers between devices  50.2 us (26%)
  local copies, waits for them, and re-layouts  10.8 us (6%)
  between operations  2.54 us (1%)
    ppermute x4, waiting for transfers between devices, shifted(): return lax.ppermute(value, axis, pairs)  24.3 us
    ppermute x8, waiting for transfers between devices, extended(): lax.ppermute(head, axis, [((i + 1) % count, i) for i in range(ends)])  24.2 us
    ppermute x8, starting transfers between devices, extended(): lax.ppermute(tail, axis, [(i, (i + 1) % count) for i in range(ends)])  22.4 us
    reduce_sum x9, other arithmetic, density_terms(): their_sum = jnp.stack([jnp.sum(dens_w, -2), jnp.sum(bond_w, -2)])  21.3 us
    ppermute x8, starting transfers between devices, extended(): lax.ppermute(head, axis, [((i + 1) % count, i) for i in range(ends)])  20.5 us
    ppermute x4, starting transfers between devices, shifted(): return lax.ppermute(value, axis, pairs)  19 us
    div x3, other arithmetic, force_terms(): weight * (bonding_slope + (slope_own[..., :, None] + slope_their[..., Non...  14.1 us
    reduce_sum x3, other arithmetic, force_terms(): return (jnp.sum(pulled, -1), -jnp.sum(pulled, -2))  9.67 us
  transfers between devices with their start and end apart: 20, of which 12 were waited for; matrix products, arithmetic and copies ran while one was open for 1% of the time, Pallas kernels for 0%

commit v1 on v0

v1 whole, which is shorter than its diff:
```python
import math

import jax
import jax.numpy as jnp
from jax import lax
from jax.experimental import pallas as pl
from jax.experimental.pallas import tpu as pltpu
from jax.sharding import PartitionSpec as P

MESH = pl.DeviceIdType.MESH

lattice_step = 3.615
cut_radius = 4.9
far_away = 1000.0

TILE_X = 2 * lattice_step
TILE_YZ = 4 * lattice_step
REACH = 3


def displacements():
    found = []
    near = lambda n: max(0.0, abs(n) * 0.5 * lattice_step - 0.7) ** 2
    for a in range(-4, 5):
        for b in range(-4, 5):
            for c in range(-4, 5):
                if (a + b + c) % 2 == 0 and (a, b, c) != (0, 0, 0):
                    if near(a) + near(b) + near(c) < cut_radius * cut_radius + 0.01:
                        found.append((a, b, c))
    return found


VECTORS = displacements()
ZS = sorted({v[2] for v in VECTORS})
BY_Z = {dz: [(v[0], v[1]) for v in VECTORS if v[2] == dz] for dz in ZS}
ORDER = {v: i for i, v in enumerate([(a, b, dz) for dz in ZS for a, b in BY_Z[dz]])}

LOG2E = 1.0 / math.log(2.0)
DECAY = 5.85 / 2.556
MORSE = 1.36
K_DENS = -DECAY * cut_radius * LOG2E
DENS_SCALE = math.exp(5.85)
K_BOND = -MORSE * cut_radius * LOG2E
C_BOND = MORSE * 2.556 * LOG2E
FOUR = 4.0 / cut_radius
BOND_SCALE = 0.5 * 0.3
PULL_BOND = -0.3 * 2.0 * MORSE
PULL_DENS = -DECAY * DENS_SCALE


def iotas():
    return (
        lax.broadcasted_iota(jnp.int32, (8, 128), 0),
        lax.broadcasted_iota(jnp.int32, (8, 128), 1),
    )


def pick(x, idx, axis):
    return jnp.take_along_axis(x, idx, axis=axis, mode="promise_in_bounds")


def turn_indices():
    row, lane = iotas()
    quarter, rest = lane // 32, lane % 32
    xs, zs = rest // 8, rest % 8
    y = (quarter - row % 4 + 4) % 4
    basis = jnp.where(xs % 2 == 0, 3 * (zs % 2), 1 + zs % 2)
    first = (xs // 2) * 64 + y * 16 + (zs // 2) * 4 + basis
    second = (row // 4) * 4 + (quarter - row % 4 + 4) % 4
    third = ((rest // 8 + row) % 4) * 32 + quarter * 8 + lane % 8
    return first, second, third


def back_indices():
    row, lane = iotas()
    quarter, rest = lane // 32, lane % 32
    first = (rest // 8) * 32 + ((quarter - row % 4 + 4) % 4) * 8 + lane % 8
    second = (row // 4) * 4 + (quarter - row % 4 + 4) % 4
    basis = lane % 4
    xs = 2 * (lane // 64) + jnp.where((basis == 1) | (basis == 2), 1, 0)
    zs = 2 * ((lane // 4) % 4) + basis // 2
    third = (((lane // 16) % 4 + row) % 4) * 32 + xs * 8 + zs
    return first, second, third


def turned(x, idx):
    return pick(pick(pick(x, idx[0], 1), idx[1], 0), idx[2], 1)


def neighbours():
    return [(a, b, c) for a in (1, -1, 0) for b in (-1, 0, 1) for c in (-1, 0, 1) if (a, b, c) != (0, 0, 0)]


NEXT = neighbours()


def gather_tiles(sizes, pos_ref, occ_ref, raw_ref, occ_v, local, send, recv):
    n_x, n_y, n_z = sizes
    me_x, me_y, me_z = (lax.axis_index(a) for a in ("gx", "gy", "gz"))

    def device(a, b, c):
        return (me_x + a, lax.rem(me_y + b + n_y, n_y), lax.rem(me_z + c + n_z, n_z))

    def grouped(act):
        for a in (1, -1, 0):
            todo = [(i, v) for i, v in enumerate(NEXT) if v[0] == a]

            def run(todo=todo):
                for i, v in todo:
                    act(i, v)

            if a == 1:
                pl.when(me_x < n_x - 1)(run)
            elif a == -1:
                pl.when(me_x > 0)(run)
            else:
                run()

    barrier = pltpu.get_barrier_semaphore()
    grouped(
        lambda i, v: pl.semaphore_signal(barrier, inc=1, device_id=device(*v), device_id_type=MESH)
    )
    get_pos = pltpu.make_async_copy(pos_ref.at[:, :, 0], raw_ref.at[:, 2:6, 5:7], local.at[0])
    get_occ = pltpu.make_async_copy(occ_ref.at[:, 0], occ_v, local.at[1])
    get_pos.start()
    get_occ.start()

    def blank(where):
        def run():
            raw_ref[:, where : where + 2] = jnp.zeros((3, 2, 16, 128), jnp.float32)

        return run

    pl.when(me_x == 0)(blank(0))
    pl.when(me_x == n_x - 1)(blank(6))
    get_occ.wait()
    get_pos.wait()
    for t in range(4):
        empty = jnp.where(occ_v[t] != 0, 0.0, far_away)
        raw_ref[0, 2 + t, 5:7] = raw_ref[0, 2 + t, 5:7] + empty
    inner = jnp.where(me_x > 0, 9, 0) + jnp.where(me_x < n_x - 1, 9, 0) + 8
    pl.semaphore_wait(barrier, inner)

    def copy(i, v):
        a, b, c = v
        x_from, x_to, x_n = {0: (2, 2, 4), 1: (4, 0, 2), -1: (2, 6, 2)}[a]
        z_from, z_to, z_n = {0: (1, 1, 2), 1: (2, 0, 1), -1: (1, 3, 1)}[c]
        row = 4 * (1 - b) + z_to
        return pltpu.make_async_remote_copy(
            src_ref=raw_ref.at[:, x_from : x_from + x_n, 4 + z_from : 4 + z_from + z_n],
            dst_ref=raw_ref.at[:, x_to : x_to + x_n, row : row + z_n],
            send_sem=send.at[i],
            recv_sem=recv.at[i],
            device_id=device(a, b, c),
            device_id_type=MESH,
        )

    grouped(lambda i, v: copy(i, v).start())

    def arrived(i, v):
        copy(i, v).wait_recv()

    def arrivals():
        for a in (1, -1, 0):
            todo = [(i, v) for i, v in enumerate(NEXT) if v[0] == a]

            def run(todo=todo):
                for i, v in todo:
                    arrived(i, v)

            if a == 1:
                pl.when(me_x > 0)(run)
            elif a == -1:
                pl.when(me_x < n_x - 1)(run)
            else:
                run()

    arrivals()
    grouped(lambda i, v: copy(i, v).wait_send())


def pair_density(centre, near):
    sep = [n - c for n, c in zip(near, centre)]
    dist_sq = sep[0] * sep[0] + sep[1] * sep[1] + sep[2] * sep[2]
    inside = jnp.maximum(1.0 - dist_sq, 0.0)
    inverse = lax.rsqrt(dist_sq)
    radius = dist_sq * inverse
    part = jnp.exp2(K_DENS * radius) * inside
    return sep, inside, inverse, radius, part


def pair_all(centre, near):
    sep, inside, inverse, radius, part = pair_density(centre, near)
    nearer = jnp.exp2(K_BOND * radius + C_BOND)
    less = nearer - 2.0
    near_in = nearer * inside
    over = inside * inverse
    pull_bond = near_in * ((nearer - 1.0) * over + (FOUR / (2.0 * MORSE)) * less)
    pull_dens = part * (over + FOUR / DECAY)
    return sep, part * inside, near_in * inside * less, pull_bond, pull_dens


def forces(
    edges, raw_ref, occ_ref, force_ref, energy_ref, tiles, halves, tiles_x, halves_x, slope, slope_half, slope_x, slope_half_x, density, bond, pull, weighted,
):
    row, lane = iotas()
    low_x, high_x, low_y, high_y, low_z, high_z = edges()
    turn = turn_indices()
    third = (lane % 32) // 8
    out_z = (low_z & (third == 0)) | (high_z & (third == 3))
    far_z = jnp.where(out_z, far_away, 0.0)
    shift_z = (third - 1).astype(jnp.float32) * TILE_YZ
    odd = (lane // 32 + lane) % 2 == 1
    unit = 1.0 / cut_radius

    for t in range(8):
        for half in range(2):
            tile_y = 2 * half + row // 4
            far = far_z + jnp.where((low_y & (tile_y == 0)) | (high_y & (tile_y == 2)), far_away, 0.0)
            if t < 2:
                far = far + jnp.where(low_x, far_away, 0.0)
            if t > 5:
                far = far + jnp.where(high_x, far_away, 0.0)
            shifts = [
                far + (t - 2) * TILE_X,
                (tile_y - 1).astype(jnp.float32) * TILE_YZ,
                shift_z,
            ]
            for c in range(3):
                v = turned(raw_ref[c, t, 8 * half : 8 * half + 8], turn)
                tiles[c, t, 8 * half : 8 * half + 8] = (v + shifts[c]) * unit

    def halved(src, dst):
        dst[0:8] = src[0:8]
        dst[1:9] = jnp.where(odd, src[0:8], src[1:9])
        dst[8:16] = jnp.where(odd, src[7:15], src[8:16])

    def halved_rows(src, dst):
        flip = odd
        dst[8:16] = jnp.where(flip, src[7:15], src[8:16])
        dst[0:8] = jnp.where(flip, pltpu.roll(src[0:8], 1, 0), src[0:8])

    for c in range(3):
        for t in range(8):
            halved_rows(tiles.at[c, t], halves.at[c, t])

    quarter = lane // 32

    def moved_x(src, dst, count):
        for half in range(2):
            rows = slice(8 * half, 8 * half + 8)
            v = [src[t, rows] for t in range(count + 2)]
            for d in range(-3, 4):
                if d == 0:
                    for t in range(count):
                        dst[3, t, rows] = v[t + 1]
                    continue
                rolled = [pltpu.roll(x, (-32 * d) % 128, 1) for x in v]
                for t in range(count):
                    if d > 0:
                        dst[d + 3, t, rows] = jnp.where(quarter + d > 3, rolled[t + 2], rolled[t + 1])
                    else:
                        dst[d + 3, t, rows] = jnp.where(quarter + d < 0, rolled[t], rolled[t + 1])

    for c in range(3):
        moved_x(tiles.at[c], tiles_x.at[c], 6)
        moved_x(halves.at[c], halves_x.at[c], 6)

    def row_of(b):
        return 2 + ((b + 1) // 2 if b % 2 else b // 2)

    def near_of(t, a, b):
        source = halves_x if b % 2 else tiles_x
        r = row_of(b)
        return [source[c, a + 3, t, r : r + 8] for c in range(3)]

    def centre_of(t, dz):
        return [pltpu.roll(tiles[c, t + 1, 2:10], dz % 128, 1) for c in range(3)]

    def home(x, dz):
        return pltpu.roll(x, (-dz) % 128, 1)

    def put_slope(t, total):
        total = total * DENS_SCALE
        value = -0.5 * lax.rsqrt(total + 0.5) + 0.004 * total
        value = jnp.where(tiles[0, t + 1, 2:10] < 0.5 * far_away / cut_radius, value, 0.0)
        zeros = jnp.zeros((8, 128), jnp.float32)
        slope[t, 0:8] = zeros
        slope[t, 8:16] = zeros
        slope[t, 2:10] = value

    def outer(k, carry):
        t = 5 * k
        total = jnp.zeros((8, 128), jnp.float32)
        for dz in ZS:
            centre = centre_of(t, dz)
            here = jnp.zeros((8, 128), jnp.float32)
            for a, b in BY_Z[dz]:
                _, inside, _, _, part = pair_density(centre, near_of(t, a, b))
                here = here + part * inside
            total = total + home(here, dz)
        put_slope(t, total)
        return carry

    lax.fori_loop(0, 2, outer, 0)

    def inner(k, carry):
        t = k + 1
        totals = [jnp.zeros((8, 128), jnp.float32)] * 8
        for dz in ZS:
            centre = centre_of(t, dz)
            here = [jnp.zeros((8, 128), jnp.float32)] * 8
            for a, b in BY_Z[dz]:
                sep, dens, bonding, pull_bond, pull_dens = pair_all(centre, near_of(t, a, b))
                here[0] = here[0] + dens
                here[1] = here[1] + bonding
                for c in range(3):
                    here[2 + c] = here[2 + c] + pull_bond * sep[c]
                    w = pull_dens * sep[c]
                    here[5 + c] = here[5 + c] + w
                    weighted[c, ORDER[a, b, dz], k] = w
            totals = [x + home(y, dz) for x, y in zip(totals, here)]
        density[k] = totals[0] * DENS_SCALE
        bond[k] = totals[1] * BOND_SCALE
        for c in range(6):
            pull[c, k] = totals[2 + c]
        put_slope(t, totals[0])
        return carry

    lax.fori_loop(0, 4, inner, 0)

    for t in range(6):
        halved_rows(slope.at[t], slope_half.at[t])
    moved_x(slope, slope_x, 4)
    moved_x(slope_half, slope_half_x, 4)

    def finish(k, carry):
        totals = [jnp.zeros((8, 128), jnp.float32)] * 3
        for dz in ZS:
            here = [jnp.zeros((8, 128), jnp.float32)] * 3
            for a, b in BY_Z[dz]:
                r = row_of(b)
                s = (slope_half_x if b % 2 else slope_x)[a + 3, k, r : r + 8]
                for c in range(3):
                    here[c] = here[c] + s * weighted[c, ORDER[a, b, dz], k]
            totals = [x + home(y, dz) for x, y in zip(totals, here)]
        own = slope[k + 1, 2:10]
        for c in range(3):
            pull[c, k] = PULL_BOND * pull[c, k] + PULL_DENS * (own * pull[3 + c, k] + totals[c])
        d = density[k]
        bond[k] = bond[k] - jnp.sqrt(d + 0.5) + 0.002 * d * d
        return carry

    lax.fori_loop(0, 4, finish, 0)

    back = back_indices()

    def native(v):
        joined = [
            jnp.where(third < 2, pltpu.roll(v[2 * h], 120, 1), pltpu.roll(v[2 * h + 1], 8, 1))
            for h in range(2)
        ]
        both = jnp.where(row < 4, pltpu.roll(joined[0], 6, 0), pltpu.roll(joined[1], 2, 0))
        return turned(both, back)

    def store(dst, v):
        for t in range(4):
            dst[t, 0] = jnp.where(occ_ref[t, 0] != 0, v[2 * t : 2 * t + 2], 0.0)

    for c in range(3):
        store(force_ref.at[c], native([pull[c, k] for k in range(4)]))
    store(energy_ref, native([bond[k] for k in range(4)]))


def vmem():
    return pl.BlockSpec(memory_space=pltpu.VMEM)


def force_scratch():
    f32 = lambda *s: pltpu.VMEM(s, jnp.float32)
    return [
        f32(3, 8, 16, 128),
        f32(3, 8, 16, 128),
        f32(3, 7, 6, 16, 128),
        f32(3, 7, 6, 16, 128),
        f32(6, 16, 128),
        f32(6, 16, 128),
        f32(7, 4, 16, 128),
        f32(7, 4, 16, 128),
        f32(4, 8, 128),
        f32(4, 8, 128),
        f32(6, 4, 8, 128),
        f32(3, len(VECTORS), 4, 8, 128),
    ]


OUT = (
    jax.ShapeDtypeStruct((3, 4, 1, 2, 128), jnp.float32),
    jax.ShapeDtypeStruct((4, 1, 2, 128), jnp.float32),
)


def solution(mesh):
    sizes = tuple(mesh.shape[a] for a in ("gx", "gy", "gz"))
    n_x, n_y, n_z = sizes

    def edges():
        x, y, z = (lax.axis_index(a) for a in ("gx", "gy", "gz"))
        return x == 0, x == n_x - 1, y == 0, y == n_y - 1, z == 0, z == n_z - 1

    def step(positions, occupied):
        raw = pl.pallas_call(
            lambda *refs: gather_tiles(sizes, *refs),
            out_shape=pltpu.VMEM((3, 8, 16, 128), jnp.float32),
            in_specs=[pl.BlockSpec(memory_space=pl.ANY)] * 2,
            out_specs=vmem(),
            scratch_shapes=[
                pltpu.VMEM((4, 2, 128), jnp.int32),
                pltpu.SemaphoreType.DMA((2,)),
                pltpu.SemaphoreType.DMA((len(NEXT),)),
                pltpu.SemaphoreType.DMA((len(NEXT),)),
            ],
            compiler_params=pltpu.CompilerParams(collective_id=0, has_side_effects=True),
        )(positions, occupied)
        raw = pltpu.with_memory_space_constraint(raw, pltpu.VMEM)
        return pl.pallas_call(
            lambda *refs: forces(edges, *refs),
            out_shape=OUT,
            in_specs=[vmem(), vmem()],
            out_specs=[vmem(), vmem()],
            scratch_shapes=force_scratch(),
            compiler_params=pltpu.CompilerParams(vmem_limit_bytes=40 * 2**20),
        )(raw, occupied)

    in_specs = (P(None, "gx", "gy", "gz", None), P("gx", "gy", "gz", None))
    out_specs = (P(None, "gx", "gy", "gz", None), P("gx", "gy", "gz", None))
    return jax.shard_map(step, mesh=mesh, in_specs=in_specs, out_specs=out_specs, check_vma=False)
```

time: 190 us -> 32.8 us (0.17)
  the two profiles are of different devices: /device:TPU:111 before, /device:TPU:1 now
where the time goes in v1:
time: 32.8 us; the launch traced here: 32.7 us
  Pallas kernels  32 us (98%)
  between operations  0.65 us (2%)
    pallas_call x1, Pallas kernels, step(): pl.pallas_call(lambda *refs: gather_tiles(sizes, *refs), out_shape=pltpu....  26.6 us
    pallas_call x1, Pallas kernels, step(): pl.pallas_call(lambda *refs: forces(edges, *refs), out_shape=OUT, in_spec...  5.35 us

profile of v1, /device:TPU:1, one launch (start us, length us, event | category | flops | bytes accessed | tf_op | source)
XLA Modules:
  0.0 32.7 jit_solution(7778690246924119369)
XLA Ops:
  0.6 0.0 copy-start
  0.6 26.6 %shard_map.41.refs_0_ = f32[3,8,16,128]{3,2,1,0:T(8,128)S(1)} custom-call(f32[3,4,1,2,128]{4,3,2,1,0:T(2,128)} %refs_0_.1, s32[4,1,2,128]{3,2,1,0:T(2,128)} %refs_1_.3), custom_call_target="tpu_custom_call" | custom-call | tf_op jit(solution)/shard_map/pallas_call | solution.py:412
  27.3 0.0 copy-done
  27.3 5.3 %shard_map.42 = (f32[3,4,1,2,128]{4,3,2,1,0:T(2,128)}, f32[4,1,2,128]{3,2,1,0:T(2,128)}) custom-call(f32[3,8,16,128]{3,2,1,0:T(8,128)S(1)} %shard_map.41.refs_0_, s32[4,1,2,128]{3,2,1,0:T(2,128)S(1)} %copy-done), custom_call_target="tpu_custom_call" | custom-call | tf_op jit(solution)/shard_map/pallas_call | solution.py:426
Async XLA Ops:
  0.6 26.7 %copy-start = (s32[4,1,2,128]{3,2,1,0:T(2,128)S(1)}, s32[4,1,2,128]{3,2,1,0:T(2,128)}, u32[]{:S(2)}) copy-start(s32[4,1,2,128]{3,2,1,0:T(2,128)} %refs_1_.3) | copy-start | bytes 12292

commit v2 on v1

v2 whole, which is shorter than its diff:
```python
import math

import jax
import jax.numpy as jnp
from jax import lax
from jax.experimental import pallas as pl
from jax.experimental.pallas import tpu as pltpu
from jax.sharding import PartitionSpec as P

MESH = pl.DeviceIdType.MESH

lattice_step = 3.615
cut_radius = 4.9
far_away = 1000.0

TILE_X = 2 * lattice_step
TILE_YZ = 4 * lattice_step
REACH = 3


def displacements():
    found = []
    near = lambda n: max(0.0, abs(n) * 0.5 * lattice_step - 0.7) ** 2
    for a in range(-4, 5):
        for b in range(-4, 5):
            for c in range(-4, 5):
                if (a + b + c) % 2 == 0 and (a, b, c) != (0, 0, 0):
                    if near(a) + near(b) + near(c) < cut_radius * cut_radius + 0.01:
                        found.append((a, b, c))
    return found


VECTORS = displacements()
ZS = sorted({v[2] for v in VECTORS})
BY_Z = {dz: [(v[0], v[1]) for v in VECTORS if v[2] == dz] for dz in ZS}
ORDER = {v: i for i, v in enumerate([(a, b, dz) for dz in ZS for a, b in BY_Z[dz]])}

LOG2E = 1.0 / math.log(2.0)
DECAY = 5.85 / 2.556
MORSE = 1.36
K_DENS = -DECAY * cut_radius * LOG2E
DENS_SCALE = math.exp(5.85)
K_BOND = -MORSE * cut_radius * LOG2E
C_BOND = MORSE * 2.556 * LOG2E
FOUR = 4.0 / cut_radius
BOND_SCALE = 0.5 * 0.3
PULL_BOND = -0.3 * 2.0 * MORSE
PULL_DENS = -DECAY * DENS_SCALE


def iotas():
    return (
        lax.broadcasted_iota(jnp.int32, (8, 128), 0),
        lax.broadcasted_iota(jnp.int32, (8, 128), 1),
    )


def pick(x, idx, axis):
    return jnp.take_along_axis(x, idx, axis=axis, mode="promise_in_bounds")


def turn_indices():
    row, lane = iotas()
    quarter, rest = lane // 32, lane % 32
    xs, zs = rest // 8, rest % 8
    y = (quarter - row % 4 + 4) % 4
    basis = jnp.where(xs % 2 == 0, 3 * (zs % 2), 1 + zs % 2)
    first = (xs // 2) * 64 + y * 16 + (zs // 2) * 4 + basis
    second = (row // 4) * 4 + (quarter - row % 4 + 4) % 4
    third = ((rest // 8 + row) % 4) * 32 + quarter * 8 + lane % 8
    return first, second, third


def back_indices():
    row, lane = iotas()
    quarter, rest = lane // 32, lane % 32
    first = (rest // 8) * 32 + ((quarter - row % 4 + 4) % 4) * 8 + lane % 8
    second = (row // 4) * 4 + (quarter - row % 4 + 4) % 4
    basis = lane % 4
    xs = 2 * (lane // 64) + jnp.where((basis == 1) | (basis == 2), 1, 0)
    zs = 2 * ((lane // 4) % 4) + basis // 2
    third = (((lane // 16) % 4 + row) % 4) * 32 + xs * 8 + zs
    return first, second, third


def turned(x, idx):
    return pick(pick(pick(x, idx[0], 1), idx[1], 0), idx[2], 1)


YZ = [(b, c) for b in (-1, 0, 1) for c in (-1, 0, 1)]
NEXT = [(a, b, c) for a in (0, 1, -1) for b, c in YZ if (a, b, c) != (0, 0, 0)]


def exchange(sizes, raw_ref, send, recv, mate_go, far_go):
    n_x, n_y, n_z = sizes
    me_x, me_y, me_z = (lax.axis_index(a) for a in ("gx", "gy", "gz"))
    inner = (me_x == 1) | (me_x == 2)
    low_pair = me_x < 2
    my_inner = jnp.where(low_pair, 1, 2)
    mate = jnp.where(low_pair, 1 - me_x, 5 - me_x)
    barrier = pltpu.get_barrier_semaphore()

    def there(b, c, sign=1):
        ok = []
        for step, me, n in ((b * sign, me_y, n_y), (c * sign, me_z, n_z)):
            if step == 1:
                ok.append(me < n - 1)
            if step == -1:
                ok.append(me > 0)
        return ok

    def when(conditions, act):
        if not conditions:
            return act()
        both = conditions[0]
        for x in conditions[1:]:
            both = both & x
        pl.when(both)(act)

    def count(steps, sign=1):
        total = 0
        for b, c in steps:
            ok = there(b, c, sign)
            if not ok:
                total = total + 1
                continue
            both = ok[0]
            for x in ok[1:]:
                both = both & x
            total = total + both.astype(jnp.int32)
        return total

    def greet(x, b, c):
        pl.semaphore_signal(
            barrier, inc=1, device_id=(x, me_y + b, me_z + c), device_id_type=MESH
        )

    around = [v for v in YZ if v != (0, 0)]

    def enter():
        far_outer = jnp.where(low_pair, 3, 0)

        def far():
            greet(mate, 0, 0)
            for b, c in YZ:
                when(there(b, c), lambda b=b, c=c: greet(far_outer, b, c))

        pl.when(inner)(far)
        pl.when(~inner)(lambda: greet(my_inner, 0, 0))
        for b, c in around:
            when(there(b, c), lambda b=b, c=c: greet(my_inner, b, c))

    def tell_mate(sem):
        pl.semaphore_signal(sem, inc=1, device_id=(mate, me_y, me_z), device_id_type=MESH)

    def copy(v):
        a, b, c = v
        i = NEXT.index(v)
        x_from, x_to, x_n = {0: (2, 2, 4), 1: (4, 0, 2), -1: (2, 6, 2)}[a]
        z_from, z_to, z_n = {0: (1, 1, 2), 1: (2, 0, 1), -1: (1, 3, 1)}[c]
        row = 4 * (1 - b) + z_to
        return pltpu.make_async_remote_copy(
            src_ref=raw_ref.at[:, x_from : x_from + x_n, 4 + z_from : 4 + z_from + z_n],
            dst_ref=raw_ref.at[:, x_to : x_to + x_n, row : row + z_n],
            send_sem=send.at[i],
            recv_sem=recv.at[i],
            device_id=(me_x + a, me_y + b, me_z + c),
            device_id_type=MESH,
        )

    def each(a, act, sign=1):
        for b, c in YZ:
            if (a, b, c) != (0, 0, 0):
                when(there(b, c, sign), lambda b=b, c=c: act(copy((a, b, c))))

    start, sent, got = (lambda x: x.start()), (lambda x: x.wait_send()), (lambda x: x.wait_recv())
    even = lax.rem(me_x, 2) == 0

    def near_all(act, sign=1):
        each(0, act, sign)
        pl.when(even == (sign == 1))(lambda: each(1, act, sign))
        pl.when(even == (sign != 1))(lambda: each(-1, act, sign))

    def far_all(act, sign=1):
        pl.when(me_x == (1 if sign == 1 else 2))(lambda: each(1, act, sign))
        pl.when(me_x == (2 if sign == 1 else 1))(lambda: each(-1, act, sign))

    def near_inner():
        pl.semaphore_wait(barrier, count(around) + count(YZ))
        tell_mate(mate_go)

    def near_outer():
        pl.semaphore_wait(mate_go, 1)

    def near():
        pl.when(inner)(near_inner)
        pl.when(~inner)(near_outer)
        near_all(start)

    def far_inner():
        pl.semaphore_wait(far_go, 1)
        far_all(start)

    def far_outer():
        pl.semaphore_wait(barrier, count(YZ) + 1)
        tell_mate(far_go)

    def far():
        pl.when(~inner)(far_outer)
        pl.when(inner)(far_inner)

    def near_got():
        near_all(got, -1)

    def far_got():
        far_all(got, -1)

    def all_sent():
        near_all(sent)
        far_all(sent)

    return enter, near, far, near_got, far_got, all_sent


def pair_density(centre, near):
    sep = [n - c for n, c in zip(near, centre)]
    dist_sq = sep[0] * sep[0] + sep[1] * sep[1] + sep[2] * sep[2]
    inside = jnp.maximum(1.0 - dist_sq, 0.0)
    inverse = lax.rsqrt(dist_sq)
    radius = dist_sq * inverse
    part = jnp.exp2(K_DENS * radius) * inside
    return sep, inside, inverse, radius, part


def pair_all(centre, near):
    sep, inside, inverse, radius, part = pair_density(centre, near)
    nearer = jnp.exp2(K_BOND * radius + C_BOND)
    less = nearer - 2.0
    near_in = nearer * inside
    over = inside * inverse
    pull_bond = near_in * ((nearer - 1.0) * over + (FOUR / (2.0 * MORSE)) * less)
    pull_dens = part * (over + FOUR / DECAY)
    return sep, part * inside, near_in * inside * less, pull_bond, pull_dens


def atoms(sizes, pos_ref, occ_ref, force_ref, energy_ref, raw, occ_v, tiles, halves, tiles_x, halves_x, slope, slope_half, slope_x, slope_half_x, density, bond, pull, weighted, local, send, recv, mate_go, far_go):
    n_x, n_y, n_z = sizes
    me_x, me_y, me_z = (lax.axis_index(a) for a in ("gx", "gy", "gz"))
    enter, near, far, near_got, far_got, all_sent = exchange(sizes, raw, send, recv, mate_go, far_go)
    enter()
    get_pos = pltpu.make_async_copy(pos_ref.at[:, :, 0], raw.at[:, 2:6, 5:7], local.at[0])
    get_occ = pltpu.make_async_copy(occ_ref.at[:, 0], occ_v, local.at[1])
    get_pos.start()
    get_occ.start()

    nothing = lambda *s: jnp.zeros(s, jnp.float32)

    def blank_x(t):
        def run():
            raw[:, t : t + 2] = nothing(3, 2, 16, 128)

        return run

    def blank_rows(rows):
        def run():
            for r in rows:
                raw[:, :, r : r + 1] = nothing(3, 8, 1, 128)

        return run

    pl.when(me_x == 0)(blank_x(0))
    pl.when(me_x == n_x - 1)(blank_x(6))
    pl.when(me_y == 0)(blank_rows((0, 1, 2, 3)))
    pl.when(me_y == n_y - 1)(blank_rows((8, 9, 10, 11)))
    pl.when(me_z == 0)(blank_rows((0, 4, 8)))
    pl.when(me_z == n_z - 1)(blank_rows((3, 7, 11)))

    get_occ.wait()
    get_pos.wait()
    for t in range(4):
        empty = jnp.where(occ_v[t] != 0, 0.0, far_away)
        raw[0, 2 + t, 5:7] = raw[0, 2 + t, 5:7] + empty

    high_pair = me_x >= 2
    waits = (me_x < 2) & (me_y < n_y // 2)
    pl.when(high_pair)(far)
    near()
    pl.when((me_x < 2) & (me_y >= n_y // 2))(far)
    near_got()

    row, lane = iotas()
    turn = turn_indices()
    third = (lane % 32) // 8
    quarter = lane // 32
    out_z = ((me_z == 0) & (third == 0)) | ((me_z == n_z - 1) & (third == 3))
    far_z = jnp.where(out_z, far_away, 0.0)
    shift_z = (third - 1).astype(jnp.float32) * TILE_YZ
    odd = (quarter + lane) % 2 == 1
    unit = 1.0 / cut_radius

    ahead = me_x < 2
    sign = jnp.where(ahead, 1, -1)

    def place(k, n):
        return jnp.where(ahead, k, n - 1 - k)

    def halved(src, dst):
        dst[8:16] = jnp.where(odd, src[7:15], src[8:16])
        dst[0:8] = jnp.where(odd, pltpu.roll(src[0:8], 1, 0), src[0:8])

    def take_tile(k, carry):
        t = place(k, 8)
        out_x = ((me_x == 0) & (t < 2)) | ((me_x == n_x - 1) & (t > 5))
        far_x = jnp.where(out_x, far_away, 0.0) + (t - 2).astype(jnp.float32) * TILE_X
        for half in range(2):
            tile_y = 2 * half + row // 4
            out_y = ((me_y == 0) & (tile_y == 0)) | ((me_y == n_y - 1) & (tile_y == 2))
            shifts = [
                far_z + jnp.where(out_y, far_away, 0.0) + far_x,
                (tile_y - 1).astype(jnp.float32) * TILE_YZ,
                shift_z,
            ]
            for c in range(3):
                v = turned(raw[c, t, 8 * half : 8 * half + 8], turn)
                tiles[c, t, 8 * half : 8 * half + 8] = (v + shifts[c]) * unit
        for c in range(3):
            halved(tiles.at[c, t], halves.at[c, t])
        return carry

    def moved_x(get, put):
        for half in range(2):
            rows = slice(8 * half, 8 * half + 8)
            v = [get(t)[rows] for t in range(3)]
            put(0)[rows] = v[1]
            for turn_by in (1, 2, 3):
                rolled = [pltpu.roll(x, 32 * turn_by, 1) for x in v]
                put(-turn_by)[rows] = jnp.where(quarter < turn_by, rolled[0], rolled[1])
                put(4 - turn_by)[rows] = jnp.where(quarter < turn_by, rolled[1], rolled[2])

    def move_tiles(k, carry):
        t = place(k, 6)
        for src, dst in ((tiles, tiles_x), (halves, halves_x)):
            for c in range(3):
                moved_x(lambda i: src.at[c, t + i], lambda d: dst.at[c, d + 3, t])
        return carry

    def move_slopes(k, carry):
        t = place(k, 6)
        for src, dst in ((slope, slope_x), (slope_half, slope_half_x)):
            moved_x(lambda i: src.at[t - 1 + i], lambda d: dst.at[d + 3, t])
        return carry

    def row_of(b):
        return 2 + ((b + 1) // 2 if b % 2 else b // 2)

    def near_of(t, a, b):
        source = halves_x if b % 2 else tiles_x
        r = row_of(b)
        return [source[c, 3 + sign * a, t, r : r + 8] for c in range(3)]

    def centre_of(t, dz):
        return [pltpu.roll(tiles[c, t + 1, 2:10], dz % 128, 1) for c in range(3)]

    def home(x, dz):
        return pltpu.roll(x, (-dz) % 128, 1)

    def put_slope(t, total):
        total = total * DENS_SCALE
        value = -0.5 * lax.rsqrt(total + 0.5) + 0.004 * total
        value = jnp.where(tiles[0, t + 1, 2:10] < 0.5 * far_away / cut_radius, value, 0.0)
        slope[t, 0:8] = nothing(8, 128)
        slope[t, 8:16] = nothing(8, 128)
        slope[t, 2:10] = value
        halved(slope.at[t], slope_half.at[t])

    def ghost_density(k):
        t = place(k, 6)
        total = nothing(8, 128)
        for dz in ZS:
            centre = centre_of(t, dz)
            here = nothing(8, 128)
            for a, b in BY_Z[dz]:
                _, inside, _, _, part = pair_density(centre, near_of(t, a, b))
                here = here + part * inside
            total = total + home(here, dz)
        put_slope(t, total)

    def own_pairs(k, wanted, add):
        t = place(k, 6)
        totals = [nothing(8, 128)] * 8
        for dz in ZS:
            centre = centre_of(t, dz)
            here = [nothing(8, 128)] * 8
            for a, b in BY_Z[dz]:
                if not wanted(a):
                    continue
                sep, dens, bonding, pull_bond, pull_dens = pair_all(centre, near_of(t, a, b))
                here[0] = here[0] + dens
                here[1] = here[1] + bonding
                for c in range(3):
                    here[2 + c] = here[2 + c] + pull_bond * sep[c]
                    w = pull_dens * sep[c]
                    here[5 + c] = here[5 + c] + w
                    weighted[c, ORDER[a, b, dz], t] = w
            totals = [x + home(y, dz) for x, y in zip(totals, here)]
        if add:
            totals = [totals[0] + density[t], totals[1] + bond[t]] + [totals[2 + c] + pull[c, t] for c in range(6)]
        density[t] = totals[0]
        bond[t] = totals[1]
        for c in range(6):
            pull[c, t] = totals[2 + c]
        return t, totals[0]

    def slope_pulls(k, wanted):
        t = place(k, 6)
        totals = [nothing(8, 128)] * 3
        for dz in ZS:
            here = [nothing(8, 128)] * 3
            for a, b in BY_Z[dz]:
                if not wanted(a):
                    continue
                r = row_of(b)
                s = (slope_half_x if b % 2 else slope_x)[3 + sign * a, t, r : r + 8]
                for c in range(3):
                    here[c] = here[c] + s * weighted[c, ORDER[a, b, dz], t]
            totals = [x + home(y, dz) for x, y in zip(totals, here)]
        for c in range(3):
            pull[3 + c, t] = pull[3 + c, t] + totals[c]

    def weigh_own(k):
        t = place(k, 6)
        own = slope[t, 2:10]
        for c in range(3):
            pull[3 + c, t] = own * pull[3 + c, t]

    every, behind, beyond = (lambda a: True), (lambda a: a <= 0), (lambda a: a > 0)

    def loop(first, last, act):
        def run(k, carry):
            act(k)
            return carry

        lax.fori_loop(first, last, run, 0)

    lax.fori_loop(0, 6, take_tile, 0)
    lax.fori_loop(0, 5, move_tiles, 0)
    ghost_density(0)

    def own_whole(k):
        t, total = own_pairs(k, every, False)
        put_slope(t, total)
        weigh_own(k)

    loop(1, 4, own_whole)
    own_pairs(4, behind, False)
    lax.fori_loop(1, 4, move_slopes, 0)
    loop(1, 3, lambda k: slope_pulls(k, every))
    slope_pulls(3, behind)

    pl.when(waits)(far)
    far_got()

    lax.fori_loop(6, 8, take_tile, 0)
    lax.fori_loop(4, 6, move_tiles, 0)
    ghost_density(5)
    t, total = own_pairs(4, beyond, True)
    put_slope(t, total)
    weigh_own(4)
    lax.fori_loop(3, 5, move_slopes, 0)
    slope_pulls(3, beyond)
    slope_pulls(4, every)

    back = back_indices()

    def native(v):
        joined = [
            jnp.where(third < 2, pltpu.roll(v[2 * h], 120, 1), pltpu.roll(v[2 * h + 1], 8, 1))
            for h in range(2)
        ]
        both = jnp.where(row < 4, pltpu.roll(joined[0], 6, 0), pltpu.roll(joined[1], 2, 0))
        return turned(both, back)

    def store(dst, v):
        for t in range(4):
            dst[t, 0] = jnp.where(occ_v[t] != 0, v[2 * t : 2 * t + 2], 0.0)

    for c in range(3):
        store(
            force_ref.at[c],
            native([PULL_BOND * pull[c, t] + PULL_DENS * pull[3 + c, t] for t in range(1, 5)]),
        )

    def energy_of(t):
        d = density[t] * DENS_SCALE
        return BOND_SCALE * bond[t] - jnp.sqrt(d + 0.5) + 0.002 * d * d

    store(energy_ref, native([energy_of(t) for t in range(1, 5)]))
    all_sent()


def put_out(force_in, energy_in, force_ref, energy_ref, sems):
    copies = [
        pltpu.make_async_copy(force_in, force_ref, sems.at[0]),
        pltpu.make_async_copy(energy_in, energy_ref, sems.at[1]),
    ]
    for x in copies:
        x.start()
    for x in copies:
        x.wait()


def scratch():
    f32 = lambda *s: pltpu.VMEM(s, jnp.float32)
    return [
        f32(3, 8, 16, 128),
        pltpu.VMEM((4, 2, 128), jnp.int32),
        f32(3, 8, 16, 128),
        f32(3, 8, 16, 128),
        f32(3, 7, 6, 16, 128),
        f32(3, 7, 6, 16, 128),
        f32(6, 16, 128),
        f32(6, 16, 128),
        f32(7, 6, 16, 128),
        f32(7, 6, 16, 128),
        f32(6, 8, 128),
        f32(6, 8, 128),
        f32(6, 6, 8, 128),
        f32(3, len(VECTORS), 6, 8, 128),
        pltpu.SemaphoreType.DMA((2,)),
        pltpu.SemaphoreType.DMA((len(NEXT),)),
        pltpu.SemaphoreType.DMA((len(NEXT),)),
        pltpu.SemaphoreType.REGULAR,
        pltpu.SemaphoreType.REGULAR,
    ]


def solution(mesh):
    sizes = tuple(mesh.shape[a] for a in ("gx", "gy", "gz"))

    def step(positions, occupied):
        positions, occupied = (pltpu.with_memory_space_constraint(x, pltpu.HBM) for x in (positions, occupied))
        found = pl.pallas_call(
            lambda *refs: atoms(sizes, *refs),
            out_shape=(pltpu.VMEM((3, 4, 1, 2, 128), jnp.float32), pltpu.VMEM((4, 1, 2, 128), jnp.float32)),
            in_specs=[pl.BlockSpec(memory_space=pl.ANY)] * 2,
            out_specs=[pl.BlockSpec(memory_space=pltpu.VMEM)] * 2,
            scratch_shapes=scratch(),
            compiler_params=pltpu.CompilerParams(
                collective_id=0, has_side_effects=True, vmem_limit_bytes=40 * 2**20
            ),
        )(positions, occupied)
        found = [pltpu.with_memory_space_constraint(x, pltpu.VMEM) for x in found]
        return pl.pallas_call(
            put_out,
            out_shape=[jax.ShapeDtypeStruct(x.shape, x.dtype) for x in found],
            in_specs=[pl.BlockSpec(memory_space=pltpu.VMEM)] * 2,
            out_specs=[pl.BlockSpec(memory_space=pl.ANY)] * 2,
            scratch_shapes=[pltpu.SemaphoreType.DMA((2,))],
        )(*found)

    in_specs = (P(None, "gx", "gy", "gz", None), P("gx", "gy", "gz", None))
    out_specs = (P(None, "gx", "gy", "gz", None), P("gx", "gy", "gz", None))
    return jax.shard_map(step, mesh=mesh, in_specs=in_specs, out_specs=out_specs, check_vma=False)
```

time: 32.8 us -> 23.5 us (0.72)
  Pallas kernels: 32 us -> 22.7 us
    pallas_call x2, Pallas kernels: 32 us -> 22.7 us  [the longest x1 22.1 us: step(): pl.pallas_call(lambda *refs: atoms(sizes, *refs), out_shape=(pltpu.VMEM((...]
where the time goes in v2:
time: 23.5 us; the launch traced here: 23.4 us
  Pallas kernels  22.7 us (97%)
  between operations  0.64 us (3%)
    pallas_call x1, Pallas kernels, step(): pl.pallas_call(lambda *refs: atoms(sizes, *refs), out_shape=(pltpu.VMEM((...  22.1 us
    pallas_call x1, Pallas kernels, step(): pl.pallas_call(put_out, out_shape=[jax.ShapeDtypeStruct(x.shape, x.dtype)...  0.62 us

profile of v2, /device:TPU:1, one launch (start us, length us, event | category | flops | bytes accessed | tf_op | source)
XLA Modules:
  0.0 23.4 jit_solution(16262288818549403327)
XLA Ops:
  0.6 22.1 %shard_map.41 = (f32[3,4,1,2,128]{4,3,2,1,0:T(2,128)S(1)}, f32[4,1,2,128]{3,2,1,0:T(2,128)S(1)}) custom-call(f32[3,4,1,2,128]{4,3,2,1,0:T(2,128)} %refs_0_.1, s32[4,1,2,128]{3,2,1,0:T(2,128)} %refs_1_.1), custom_call_target="tpu_custom_call" | custom-call | tf_op jit(solution)/shard_map/pallas_call | solution.py:542
  22.7 0.6 %shard_map.42 = (f32[3,4,1,2,128]{4,3,2,1,0:T(2,128)}, f32[4,1,2,128]{3,2,1,0:T(2,128)}) custom-call(f32[3,4,1,2,128]{4,3,2,1,0:T(2,128)S(1)} %get-tuple-element.4.force_in, f32[4,1,2,128]{3,2,1,0:T(2,128)S(1)} %get-tuple-element.5.energy_in), custom_call_target="tpu_custom_call" | custom-call | tf_op jit(solution)/shard_map/pallas_call | solution.py:553

commit v3 on v2

v3 whole, which is shorter than its diff:
```python
import math

import jax
import jax.numpy as jnp
from jax import lax
from jax.experimental import pallas as pl
from jax.experimental.pallas import tpu as pltpu
from jax.sharding import PartitionSpec as P

MESH = pl.DeviceIdType.MESH

lattice_step = 3.615
cut_radius = 4.9
far_away = 1000.0

TILE_X = 2 * lattice_step
TILE_YZ = 4 * lattice_step
REACH = 3


def displacements():
    found = []
    near = lambda n: max(0.0, abs(n) * 0.5 * lattice_step - 0.7) ** 2
    for a in range(-4, 5):
        for b in range(-4, 5):
            for c in range(-4, 5):
                if (a + b + c) % 2 == 0 and (a, b, c) != (0, 0, 0):
                    if near(a) + near(b) + near(c) < cut_radius * cut_radius + 0.01:
                        found.append((a, b, c))
    return found


VECTORS = displacements()
ZS = sorted({v[2] for v in VECTORS})
BY_Z = {dz: [(v[0], v[1]) for v in VECTORS if v[2] == dz] for dz in ZS}
ORDER = {v: i for i, v in enumerate([(a, b, dz) for dz in ZS for a, b in BY_Z[dz]])}

LOG2E = 1.0 / math.log(2.0)
DECAY = 5.85 / 2.556
MORSE = 1.36
K_DENS = -DECAY * cut_radius * LOG2E
DENS_SCALE = math.exp(5.85)
K_BOND = -MORSE * cut_radius * LOG2E
C_BOND = MORSE * 2.556 * LOG2E
FOUR = 4.0 / cut_radius
BOND_SCALE = 0.5 * 0.3
PULL_BOND = -0.3 * 2.0 * MORSE
PULL_DENS = -DECAY * DENS_SCALE


def iotas():
    return (
        lax.broadcasted_iota(jnp.int32, (8, 128), 0),
        lax.broadcasted_iota(jnp.int32, (8, 128), 1),
    )


def pick(x, idx, axis):
    return jnp.take_along_axis(x, idx, axis=axis, mode="promise_in_bounds")


def turn_indices():
    row, lane = iotas()
    quarter, rest = lane // 32, lane % 32
    xs, zs = rest // 8, rest % 8
    y = (quarter - row % 4 + 4) % 4
    basis = jnp.where(xs % 2 == 0, 3 * (zs % 2), 1 + zs % 2)
    first = (xs // 2) * 64 + y * 16 + (zs // 2) * 4 + basis
    second = (row // 4) * 4 + (quarter - row % 4 + 4) % 4
    third = ((rest // 8 + row) % 4) * 32 + quarter * 8 + lane % 8
    return first, second, third


def back_indices():
    row, lane = iotas()
    quarter, rest = lane // 32, lane % 32
    part = (quarter - row + 10) % 4
    first = (rest // 8) * 32 + (part % 2 + 1) * 8 + lane % 8
    second = 2 + (quarter - row % 4 + 4) % 4
    basis = lane % 4
    xs = 2 * (lane // 64) + jnp.where((basis == 1) | (basis == 2), 1, 0)
    zs = 2 * ((lane // 4) % 4) + basis // 2
    third = (((lane // 16) % 4 + row) % 4) * 32 + xs * 8 + zs
    return part < 2, first, second, third


def turned(x, idx):
    return pick(pick(pick(x, idx[0], 1), idx[1], 0), idx[2], 1)


YZ = sorted(((b, c) for b in (-1, 0, 1) for c in (-1, 0, 1)), key=lambda v: -abs(v[0]) - abs(v[1]))
NEXT = [(a, b, c) for a in (0, 1, -1) for b, c in YZ if (a, b, c) != (0, 0, 0)]


def exchange(sizes, raw_ref, send, recv, near_go):
    n_x, n_y, n_z = sizes
    me_x, me_y, me_z = (lax.axis_index(a) for a in ("gx", "gy", "gz"))
    inner = (me_x == 1) | (me_x == 2)
    low_pair = me_x < 2
    my_outer = jnp.where(low_pair, 0, 3)
    mate = jnp.where(low_pair, 1 - me_x, 5 - me_x)
    barrier = pltpu.get_barrier_semaphore()

    def there(b, c, sign=1):
        ok = []
        for step, me, n in ((b * sign, me_y, n_y), (c * sign, me_z, n_z)):
            if step == 1:
                ok.append(me < n - 1)
            if step == -1:
                ok.append(me > 0)
        return ok

    def when(conditions, act):
        if not conditions:
            return act()
        both = conditions[0]
        for x in conditions[1:]:
            both = both & x
        pl.when(both)(act)

    def count(steps):
        total = 0
        for b, c in steps:
            ok = there(b, c)
            if not ok:
                total = total + 1
                continue
            both = ok[0]
            for x in ok[1:]:
                both = both & x
            total = total + both.astype(jnp.int32)
        return total

    def greet(x, b, c):
        pl.semaphore_signal(
            barrier, inc=1, device_id=(x, me_y + b, me_z + c), device_id_type=MESH
        )

    around = [v for v in YZ if v != (0, 0)]

    def enter():
        def as_inner():
            for b, c in YZ:
                when(there(b, c), lambda b=b, c=c: greet(3 - me_x, b, c))
            greet(mate, 0, 0)

        pl.when(inner)(as_inner)
        for b, c in around:
            when(there(b, c), lambda b=b, c=c: greet(my_outer, b, c))

    def copy(v):
        a, b, c = v
        i = NEXT.index(v)
        x_from, x_to, x_n = {0: (2, 2, 4), 1: (4, 0, 2), -1: (2, 6, 2)}[a]
        z_from, z_to, z_n = {0: (1, 1, 2), 1: (2, 0, 1), -1: (1, 3, 1)}[c]
        row = 4 * (1 - b) + z_to
        return pltpu.make_async_remote_copy(
            src_ref=raw_ref.at[:, x_from : x_from + x_n, 4 + z_from : 4 + z_from + z_n],
            dst_ref=raw_ref.at[:, x_to : x_to + x_n, row : row + z_n],
            send_sem=send.at[i],
            recv_sem=recv.at[i],
            device_id=(me_x + a, me_y + b, me_z + c),
            device_id_type=MESH,
        )

    def each(a, act, sign=1):
        for b, c in YZ:
            if (a, b, c) != (0, 0, 0):
                when(there(b, c, sign), lambda b=b, c=c: act(copy((a, b, c))))

    start, sent, got = (lambda x: x.start()), (lambda x: x.wait_send()), (lambda x: x.wait_recv())
    even = lax.rem(me_x, 2) == 0

    def near_all(act, sign=1):
        each(0, act, sign)
        pl.when(even == (sign == 1))(lambda: each(1, act, sign))
        pl.when(even == (sign != 1))(lambda: each(-1, act, sign))

    def far_all(act, sign=1):
        pl.when(me_x == (1 if sign == 1 else 2))(lambda: each(1, act, sign))
        pl.when(me_x == (2 if sign == 1 else 1))(lambda: each(-1, act, sign))

    def far_inner():
        pl.semaphore_wait(barrier, count(YZ))
        far_all(start)

    def far():
        pl.when(inner)(far_inner)

    def near_outer():
        pl.semaphore_wait(barrier, count(around) + count(YZ))
        pl.semaphore_signal(near_go, inc=1, device_id=(mate, me_y, me_z), device_id_type=MESH)

    def near():
        pl.when(~inner)(near_outer)
        pl.when(inner)(lambda: pl.semaphore_wait(near_go, 1))
        near_all(start)

    def near_got():
        near_all(got, -1)

    def far_got():
        far_all(got, -1)

    def all_sent():
        near_all(sent)
        far_all(sent)

    return enter, near, far, near_got, far_got, all_sent


def pair_density(centre, near):
    sep = [n - c for n, c in zip(near, centre)]
    dist_sq = sep[0] * sep[0] + sep[1] * sep[1] + sep[2] * sep[2]
    inside = jnp.maximum(1.0 - dist_sq, 0.0)
    inverse = lax.rsqrt(dist_sq)
    radius = dist_sq * inverse
    part = jnp.exp2(K_DENS * radius) * inside
    return sep, inside, inverse, radius, part


def pair_all(centre, near):
    sep, inside, inverse, radius, part = pair_density(centre, near)
    nearer = jnp.exp2(K_BOND * radius + C_BOND)
    less = nearer - 2.0
    near_in = nearer * inside
    over = inside * inverse
    pull_bond = near_in * ((nearer - 1.0) * over + (FOUR / (2.0 * MORSE)) * less)
    pull_dens = part * (over + FOUR / DECAY)
    return sep, part * inside, near_in * inside * less, pull_bond, pull_dens


def atoms(sizes, pos_ref, occ_ref, force_ref, energy_ref, raw, occ_v, tiles, rolled, moved, centres, slope, slope_rolled, slope_moved, density, bond, pull, weighted, local, send, recv, near_go):
    n_x, n_y, n_z = sizes
    me_x, me_y, me_z = (lax.axis_index(a) for a in ("gx", "gy", "gz"))
    enter, near, far, near_got, far_got, all_sent = exchange(sizes, raw, send, recv, near_go)
    get_pos = pltpu.make_async_copy(pos_ref.at[:, :, 0], raw.at[:, 2:6, 5:7], local.at[0])
    get_occ = pltpu.make_async_copy(occ_ref.at[:, 0], occ_v, local.at[1])
    get_pos.start()
    get_occ.start()
    enter()

    nothing = lambda *s: jnp.zeros(s, jnp.float32)

    def blank_x(t):
        def run():
            raw[:, t : t + 2] = nothing(3, 2, 16, 128)

        return run

    def blank_rows(rows):
        def run():
            for r in rows:
                raw[:, :, r : r + 1] = nothing(3, 8, 1, 128)

        return run

    get_occ.wait()
    get_pos.wait()
    for t in range(4):
        empty = jnp.where(occ_v[t] != 0, 0.0, far_away)
        raw[0, 2 + t, 5:7] = raw[0, 2 + t, 5:7] + empty

    ahead = me_x < 2
    long_ahead = me_y < (5 * n_y) // 8
    pl.when(~ahead)(far)
    near()

    pl.when(me_x == 0)(blank_x(0))
    pl.when(me_x == n_x - 1)(blank_x(6))
    pl.when(me_y == 0)(blank_rows((0, 1, 2, 3)))
    pl.when(me_y == n_y - 1)(blank_rows((8, 9, 10, 11)))
    pl.when(me_z == 0)(blank_rows((0, 4, 8)))
    pl.when(me_z == n_z - 1)(blank_rows((3, 7, 11)))

    row, lane = iotas()
    turn = turn_indices()
    third = (lane % 32) // 8
    quarter = lane // 32
    out_z = ((me_z == 0) & (third == 0)) | ((me_z == n_z - 1) & (third == 3))
    far_z = jnp.where(out_z, far_away, 0.0)
    shift_z = (third - 1).astype(jnp.float32) * TILE_YZ
    odds = [(quarter + lane + a) % 2 == 1 for a in (0, 1)]
    unit = 1.0 / cut_radius

    reach = jnp.where(ahead, quarter, 3 - quarter)

    def place(k, n):
        return jnp.where(ahead, k, n - 1 - k)

    near_got()

    def take_tile(k):
        t = place(k, 8)
        out_x = ((me_x == 0) & (t < 2)) | ((me_x == n_x - 1) & (t > 5))
        far_x = jnp.where(out_x, far_away, 0.0) + (t - 2).astype(jnp.float32) * TILE_X
        for half in range(2):
            rows = slice(8 * half, 8 * half + 8)
            tile_y = 2 * half + row // 4
            out_y = ((me_y == 0) & (tile_y == 0)) | ((me_y == n_y - 1) & (tile_y == 2))
            shifts = [
                far_z + jnp.where(out_y, far_away, 0.0) + far_x,
                (tile_y - 1).astype(jnp.float32) * TILE_YZ,
                shift_z,
            ]
            for c in range(3):
                v = (turned(raw[c, t, rows], turn) + shifts[c]) * unit
                tiles[c, k, rows] = v
                roll_planes(v, lambda a: rolled.at[c, a, k, rows])

    def roll_planes(v, put):
        for m in (1, 2, 3):
            put(jnp.where(ahead, 4 - m, m))[...] = pltpu.roll(v, 32 * m, 1)

    def crossing(a):
        return reach + a > 3 if a > 0 else reach + a < 0

    def move_tile(k, shifts):
        for a in shifts:
            for c in range(3):
                for half in range(2):
                    rows = slice(8 * half, 8 * half + 8)
                    other = k + 2 if a > 0 else k
                    moved[c, a + 3, k, rows] = jnp.where(
                        crossing(a), rolled[c, a % 4, other, rows], rolled[c, a % 4, k + 1, rows]
                    )

    def roll_slope(k, value):
        slope[k, 2:10] = value
        roll_planes(value, lambda a: slope_rolled.at[a, k])

    def move_slope(k, shifts):
        for a in shifts:
            other = k + 1 if a > 0 else k - 1
            slope_moved[a + 3, k, 2:10] = jnp.where(
                crossing(a), slope_rolled[a % 4, other], slope_rolled[a % 4, k]
            )

    def rows_of(get, a, b):
        if b % 2 == 0:
            r = 2 + b // 2
            return [x[r : r + 8] for x in get]
        r = 2 + (b + 1) // 2
        return [jnp.where(odds[a % 2], x[r - 1 : r + 7], x[r : r + 8]) for x in get]

    def near_of(k, a, b):
        return rows_of([moved.at[c, a + 3, k] if a else tiles.at[c, k + 1] for c in range(3)], a, b)

    def slope_of(k, a, b):
        return rows_of([slope_moved.at[a + 3, k] if a else slope.at[k]], a, b)[0]

    def centre_of(k, dz):
        return [pltpu.roll(tiles[c, k + 1, 2:10], dz % 128, 1) if dz else tiles[c, k + 1, 2:10] for c in range(3)]

    def home(x, dz):
        return pltpu.roll(x, (-dz) % 128, 1) if dz else x

    def slope_value(k, total):
        total = total * DENS_SCALE
        value = -0.5 * lax.rsqrt(total + 0.5) + 0.004 * total
        return jnp.where(tiles[0, k + 1, 2:10] < 0.5 * far_away / cut_radius, value, 0.0)

    def ghost_density(k):
        total = nothing(8, 128)
        for dz in ZS:
            centre = centre_of(k, dz)
            here = nothing(8, 128)
            for a, b in BY_Z[dz]:
                _, inside, _, _, part = pair_density(centre, near_of(k, a, b))
                here = here + part * inside
            total = total + home(here, dz)
        return total

    def own_pairs(k, wanted, centre_at):
        totals = [nothing(8, 128)] * 8
        for dz in ZS:
            centre = centre_at(dz)
            here = [nothing(8, 128)] * 8
            for a, b in BY_Z[dz]:
                if not wanted(a):
                    continue
                sep, dens, bonding, pull_bond, pull_dens = pair_all(centre, near_of(k, a, b))
                here[0] = here[0] + dens
                here[1] = here[1] + bonding
                for c in range(3):
                    here[2 + c] = here[2 + c] + pull_bond * sep[c]
                    w = pull_dens * sep[c]
                    here[5 + c] = here[5 + c] + w
                    weighted[c, ORDER[a, b, dz], k] = w
            totals = [x + home(y, dz) for x, y in zip(totals, here)]
        return totals

    def slope_pulls(k, wanted):
        totals = [nothing(8, 128)] * 3
        for dz in ZS:
            here = [nothing(8, 128)] * 3
            for a, b in BY_Z[dz]:
                if not wanted(a):
                    continue
                s = slope_of(k, a, b)
                for c in range(3):
                    here[c] = here[c] + s * weighted[c, ORDER[a, b, dz], k]
            totals = [x + home(y, dz) for x, y in zip(totals, here)]
        return totals

    def keep(k, totals, value):
        density[k] = totals[0]
        bond[k] = totals[1]
        for c in range(3):
            pull[c, k] = PULL_BOND * totals[2 + c] + PULL_DENS * (value * totals[5 + c])

    def add_pulls(k, totals):
        for c in range(3):
            pull[c, k] = pull[c, k] + PULL_DENS * totals[c]

    every, behind, beyond = (lambda a: True), (lambda a: a <= 0), (lambda a: a > 0)
    both_ways = (-3, -2, -1, 1, 2, 3)

    def loop(first, last, act):
        def run(k, carry):
            act(k)
            return carry

        lax.fori_loop(first, last, run, 0)

    slope[...] = nothing(6, 16, 128)
    slope_moved[...] = nothing(7, 6, 16, 128)
    loop(0, 6, take_tile)
    pl.when(ahead & ~long_ahead)(far)
    loop(0, 4, lambda k: move_tile(k, both_ways))
    move_tile(4, (-3, -2, -1))
    roll_slope(0, slope_value(0, ghost_density(0)))

    def own_whole(k):
        totals = own_pairs(k, every, lambda dz: centre_of(k, dz))
        value = slope_value(k, totals[0])
        keep(k, totals, value)
        roll_slope(k, value)

    loop(1, 4, own_whole)
    loop(1, 3, lambda k: move_slope(k, both_ways))
    move_slope(3, (-3, -2, -1))
    loop(1, 3, lambda k: add_pulls(k, slope_pulls(k, every)))
    add_pulls(3, slope_pulls(3, behind))
    for i, dz in enumerate(ZS):
        v = centre_of(4, dz)
        for c in range(3):
            centres[c, i] = v[c]

    def kept(dz):
        return [centres[c, ZS.index(dz)] for c in range(3)]

    part = own_pairs(4, behind, kept)
    density[4] = part[0]
    bond[4] = part[1]
    for c in range(6):
        pull[c + 4, 4] = part[2 + c]

    pl.when(ahead & long_ahead)(far)
    far_got()

    for k in (6, 7):
        take_tile(k)
    move_tile(4, (1, 2, 3))
    totals = own_pairs(4, beyond, kept)
    totals = [totals[0] + density[4], totals[1] + bond[4]] + [totals[2 + c] + pull[c + 4, 4] for c in range(6)]
    value = slope_value(4, totals[0])
    keep(4, totals, value)
    roll_slope(4, value)
    move_tile(5, both_ways)
    roll_slope(5, slope_value(5, ghost_density(5)))
    move_slope(3, (1, 2, 3))
    move_slope(4, both_ways)
    add_pulls(3, slope_pulls(3, beyond))
    add_pulls(4, slope_pulls(4, every))

    first_part, back, back_rows, back_slots = back_indices()

    def native(at):
        v = [at(place(p, 4) + 1) for p in range(4)]
        v = [pick(x, back, 1) for x in v]
        v = [jnp.where(first_part, v[2 * h], v[2 * h + 1]) for h in range(2)]
        v = [pick(x, back_rows, 0) for x in v]
        return pick(jnp.where(row < 4, v[0], v[1]), back_slots, 1)

    def store(dst, v):
        for t in range(4):
            dst[t, 0] = jnp.where(occ_v[t] != 0, v[2 * t : 2 * t + 2], 0.0)

    for c in range(3):
        store(force_ref.at[c], native(lambda k: pull[c, k]))

    def energy_of(k):
        d = density[k] * DENS_SCALE
        return BOND_SCALE * bond[k] - jnp.sqrt(d + 0.5) + 0.002 * d * d

    store(energy_ref, native(energy_of))
    all_sent()


def put_out(force_in, energy_in, force_ref, energy_ref, sems):
    copies = [
        pltpu.make_async_copy(force_in, force_ref, sems.at[0]),
        pltpu.make_async_copy(energy_in, energy_ref, sems.at[1]),
    ]
    for x in copies:
        x.start()
    for x in copies:
        x.wait()


def scratch():
    f32 = lambda *s: pltpu.VMEM(s, jnp.float32)
    return [
        f32(3, 8, 16, 128),
        pltpu.VMEM((4, 2, 128), jnp.int32),
        f32(3, 8, 16, 128),
        f32(3, 4, 8, 16, 128),
        f32(3, 7, 6, 16, 128),
        f32(3, len(ZS), 8, 128),
        f32(6, 16, 128),
        f32(4, 6, 8, 128),
        f32(7, 6, 16, 128),
        f32(6, 8, 128),
        f32(6, 8, 128),
        f32(10, 6, 8, 128),
        f32(3, len(VECTORS), 6, 8, 128),
        pltpu.SemaphoreType.DMA((2,)),
        pltpu.SemaphoreType.DMA((len(NEXT),)),
        pltpu.SemaphoreType.DMA((len(NEXT),)),
        pltpu.SemaphoreType.REGULAR,
    ]


def solution(mesh):
    sizes = tuple(mesh.shape[a] for a in ("gx", "gy", "gz"))

    def step(positions, occupied):
        positions, occupied = (pltpu.with_memory_space_constraint(x, pltpu.HBM) for x in (positions, occupied))
        found = pl.pallas_call(
            lambda *refs: atoms(sizes, *refs),
            out_shape=(pltpu.VMEM((3, 4, 1, 2, 128), jnp.float32), pltpu.VMEM((4, 1, 2, 128), jnp.float32)),
            in_specs=[pl.BlockSpec(memory_space=pl.ANY)] * 2,
            out_specs=[pl.BlockSpec(memory_space=pltpu.VMEM)] * 2,
            scratch_shapes=scratch(),
            compiler_params=pltpu.CompilerParams(
                collective_id=0, has_side_effects=True, vmem_limit_bytes=40 * 2**20
            ),
        )(positions, occupied)
        found = [pltpu.with_memory_space_constraint(x, pltpu.VMEM) for x in found]
        return pl.pallas_call(
            put_out,
            out_shape=[jax.ShapeDtypeStruct(x.shape, x.dtype) for x in found],
            in_specs=[pl.BlockSpec(memory_space=pltpu.VMEM)] * 2,
            out_specs=[pl.BlockSpec(memory_space=pl.ANY)] * 2,
            scratch_shapes=[pltpu.SemaphoreType.DMA((2,))],
        )(*found)

    in_specs = (P(None, "gx", "gy", "gz", None), P("gx", "gy", "gz", None))
    out_specs = (P(None, "gx", "gy", "gz", None), P("gx", "gy", "gz", None))
    return jax.shard_map(step, mesh=mesh, in_specs=in_specs, out_specs=out_specs, check_vma=False)
```

time: 23.5 us -> 22.5 us (0.957)
  Pallas kernels: 22.7 us -> 21.7 us
    pallas_call x1, Pallas kernels: 22.1 us -> 21.1 us  [step(): pl.pallas_call(lambda *refs: atoms(sizes, *refs), out_shape=(pltpu.VMEM((...]
where the time goes in v3:
time: 22.5 us; the launch traced here: 22.4 us
  Pallas kernels  21.7 us (96%)
  between operations  0.64 us (3%)
    pallas_call x1, Pallas kernels, step(): pl.pallas_call(lambda *refs: atoms(sizes, *refs), out_shape=(pltpu.VMEM((...  21.1 us
    pallas_call x1, Pallas kernels, step(): pl.pallas_call(put_out, out_shape=[jax.ShapeDtypeStruct(x.shape, x.dtype)...  0.62 us

profile of v3, /device:TPU:1, one launch (start us, length us, event | category | flops | bytes accessed | tf_op | source)
XLA Modules:
  0.0 22.4 jit_solution(5946832567556504436)
XLA Ops:
  0.6 21.1 %shard_map.41 = (f32[3,4,1,2,128]{4,3,2,1,0:T(2,128)S(1)}, f32[4,1,2,128]{3,2,1,0:T(2,128)S(1)}) custom-call(f32[3,4,1,2,128]{4,3,2,1,0:T(2,128)} %refs_0_.1, s32[4,1,2,128]{3,2,1,0:T(2,128)} %refs_1_.1), custom_call_target="tpu_custom_call" | custom-call | tf_op jit(solution)/shard_map/pallas_call | solution.py:540
  21.8 0.6 %shard_map.42 = (f32[3,4,1,2,128]{4,3,2,1,0:T(2,128)}, f32[4,1,2,128]{3,2,1,0:T(2,128)}) custom-call(f32[3,4,1,2,128]{4,3,2,1,0:T(2,128)S(1)} %get-tuple-element.4.force_in, f32[4,1,2,128]{3,2,1,0:T(2,128)S(1)} %get-tuple-element.5.energy_in), custom_call_target="tpu_custom_call" | custom-call | tf_op jit(solution)/shard_map/pallas_call | solution.py:551

commit v4 on v3

--- a/solution.py
+++ b/solution.py
@@ -67,8 +67,7 @@
     basis = jnp.where(xs % 2 == 0, 3 * (zs % 2), 1 + zs % 2)
     first = (xs // 2) * 64 + y * 16 + (zs // 2) * 4 + basis
     second = (row // 4) * 4 + (quarter - row % 4 + 4) % 4
-    third = ((rest // 8 + row) % 4) * 32 + quarter * 8 + lane % 8
-    return first, second, third
+    return first, second
 
 
 def back_indices():
@@ -82,10 +81,6 @@
     zs = 2 * ((lane // 4) % 4) + basis // 2
     third = (((lane // 16) % 4 + row) % 4) * 32 + xs * 8 + zs
     return part < 2, first, second, third
-
-
-def turned(x, idx):
-    return pick(pick(pick(x, idx[0], 1), idx[1], 0), idx[2], 1)
 
 
 YZ = sorted(((b, c) for b in (-1, 0, 1) for c in (-1, 0, 1)), key=lambda v: -abs(v[0]) - abs(v[1]))
@@ -164,7 +159,7 @@
         )
 
     def each(a, act, sign=1):
-        for b, c in YZ:
+        for b, c in YZ if sign == 1 else YZ[::-1]:
             if (a, b, c) != (0, 0, 0):
                 when(there(b, c, sign), lambda b=b, c=c: act(copy((a, b, c))))
 
@@ -230,7 +225,7 @@
     return sep, part * inside, near_in * inside * less, pull_bond, pull_dens
 
 
-def atoms(sizes, pos_ref, occ_ref, force_ref, energy_ref, raw, occ_v, tiles, rolled, moved, centres, slope, slope_rolled, slope_moved, density, bond, pull, weighted, local, send, recv, near_go):
+def atoms(sizes, pos_ref, occ_ref, force_ref, energy_ref, raw, occ_v, rolled, moved, centres, slope, slope_rolled, slope_moved, density, bond, pull, edge_bonds, weighted, local, send, recv, near_go):
     n_x, n_y, n_z = sizes
     me_x, me_y, me_z = (lax.axis_index(a) for a in ("gx", "gy", "gz"))
     enter, near, far, near_got, far_got, all_sent = exchange(sizes, raw, send, recv, near_go)
@@ -238,7 +233,32 @@
     get_occ = pltpu.make_async_copy(occ_ref.at[:, 0], occ_v, local.at[1])
     get_pos.start()
     get_occ.start()
-    enter()
+
+    def load():
+        get_occ.wait()
+        get_pos.wait()
+        for t in range(4):
+            empty = jnp.where(occ_v[t] != 0, 0.0, far_away)
+            raw[0, 2 + t, 5:7] = raw[0, 2 + t, 5:7] + empty
+
+    ahead = me_x < 2
+    most = me_y < n_y // 2
+    least = me_y >= (5 * n_y) // 8
+    at_once = (me_x == 2) & most
+
+    def send_first():
+        load()
+        far()
+        enter()
+
+    def greet_first():
+        enter()
+        load()
+
+    pl.when(at_once)(send_first)
+    pl.when(~at_once)(greet_first)
+    pl.when(~ahead & ~most)(far)
+    near()
 
     nothing = lambda *s: jnp.zeros(s, jnp.float32)
 
@@ -254,17 +274,6 @@
                 raw[:, :, r : r + 1] = nothing(3, 8, 1, 128)
 
         return run
-
-    get_occ.wait()
-    get_pos.wait()
-    for t in range(4):
-        empty = jnp.where(occ_v[t] != 0, 0.0, far_away)
-        raw[0, 2 + t, 5:7] = raw[0, 2 + t, 5:7] + empty
-
-    ahead = me_x < 2
-    long_ahead = me_y < (5 * n_y) // 8
-    pl.when(~ahead)(far)
-    near()
 
     pl.when(me_x == 0)(blank_x(0))
     pl.when(me_x == n_x - 1)(blank_x(6))
@@ -287,6 +296,8 @@
 
     def place(k, n):
         return jnp.where(ahead, k, n - 1 - k)
+
+    planes = [((third + row) % 4) * 32 + ((quarter + jnp.where(ahead, a, 4 - a)) % 4) * 8 + lane % 8 for a in range(4)]
 
     near_got()
 
@@ -304,13 +315,15 @@
                 shift_z,
             ]
             for c in range(3):
-                v = (turned(raw[c, t, rows], turn) + shifts[c]) * unit
-                tiles[c, k, rows] = v
-                roll_planes(v, lambda a: rolled.at[c, a, k, rows])
+                v = pick(pick(raw[c, t, rows], turn[0], 1), turn[1], 0)
+                for a in range(4):
+                    rolled[c, a, k, rows] = (pick(v, planes[a], 1) + shifts[c]) * unit
 
     def roll_planes(v, put):
-        for m in (1, 2, 3):
-            put(jnp.where(ahead, 4 - m, m))[...] = pltpu.roll(v, 32 * m, 1)
+        back, half, on = (pltpu.roll(v, 32 * m, 1) for m in (1, 2, 3))
+        put(1)[...] = jnp.where(ahead, on, back)
+        put(2)[...] = half
+        put(3)[...] = jnp.where(ahead, back, on)
 
     def crossing(a):
         return reach + a > 3 if a > 0 else reach + a < 0
@@ -344,13 +357,13 @@
         return [jnp.where(odds[a % 2], x[r - 1 : r + 7], x[r : r + 8]) for x in get]
 
     def near_of(k, a, b):
-        return rows_of([moved.at[c, a + 3, k] if a else tiles.at[c, k + 1] for c in range(3)], a, b)
+        return rows_of([moved.at[c, a + 3, k] if a else rolled.at[c, 0, k + 1] for c in range(3)], a, b)
 
     def slope_of(k, a, b):
         return rows_of([slope_moved.at[a + 3, k] if a else slope.at[k]], a, b)[0]
 
     def centre_of(k, dz):
-        return [pltpu.roll(tiles[c, k + 1, 2:10], dz % 128, 1) if dz else tiles[c, k + 1, 2:10] for c in range(3)]
+        return [pltpu.roll(rolled[c, 0, k + 1, 2:10], dz % 128, 1) if dz else rolled[c, 0, k + 1, 2:10] for c in range(3)]
 
     def home(x, dz):
         return pltpu.roll(x, (-dz) % 128, 1) if dz else x
@@ -358,7 +371,7 @@
     def slope_value(k, total):
         total = total * DENS_SCALE
         value = -0.5 * lax.rsqrt(total + 0.5) + 0.004 * total
-        return jnp.where(tiles[0, k + 1, 2:10] < 0.5 * far_away / cut_radius, value, 0.0)
+        return jnp.where(rolled[0, 0, k + 1, 2:10] < 0.5 * far_away / cut_radius, value, 0.0)
 
     def ghost_density(k):
         total = nothing(8, 128)
@@ -371,14 +384,12 @@
             total = total + home(here, dz)
         return total
 
-    def own_pairs(k, wanted, centre_at):
+    def own_pairs(k):
         totals = [nothing(8, 128)] * 8
         for dz in ZS:
-            centre = centre_at(dz)
+            centre = centre_of(k, dz)
             here = [nothing(8, 128)] * 8
             for a, b in BY_Z[dz]:
-                if not wanted(a):
-                    continue
                 sep, dens, bonding, pull_bond, pull_dens = pair_all(centre, near_of(k, a, b))
                 here[0] = here[0] + dens
                 here[1] = here[1] + bonding
@@ -389,6 +400,42 @@
                     weighted[c, ORDER[a, b, dz], k] = w
             totals = [x + home(y, dz) for x, y in zip(totals, here)]
         return totals
+
+    def edge_pairs(wanted, add):
+        totals = [nothing(8, 128)] * 2
+        for i, dz in enumerate(ZS):
+            centre = [centres[c, i] for c in range(3)]
+            here = [nothing(8, 128)] * 2
+            bonds = [edge_bonds[c, i] if add else nothing(8, 128) for c in range(3)]
+            for a, b in BY_Z[dz]:
+                if not wanted(a):
+                    continue
+                sep, dens, bonding, pull_bond, pull_dens = pair_all(centre, near_of(4, a, b))
+                here = [here[0] + dens, here[1] + bonding]
+                for c in range(3):
+                    bonds[c] = bonds[c] + pull_bond * sep[c]
+                    weighted[c, ORDER[a, b, dz], 4] = pull_dens * sep[c]
+            totals = [x + home(y, dz) for x, y in zip(totals, here)]
+            for c in range(3):
+                edge_bonds[c, i] = bonds[c]
+        if add:
+            totals = [totals[0] + density[4], totals[1] + bond[4]]
+        density[4], bond[4] = totals
+        return totals[0]
+
+    def edge_pulls(value):
+        totals = [nothing(8, 128)] * 3
+        for i, dz in enumerate(ZS):
+            own = pltpu.roll(value, dz % 128, 1) if dz else value
+            here = [nothing(8, 128)] * 3
+            for a, b in BY_Z[dz]:
+                both = own + slope_of(4, a, b)
+                for c in range(3):
+                    here[c] = here[c] + both * weighted[c, ORDER[a, b, dz], 4]
+            for c in range(3):
+                totals[c] = totals[c] + home(PULL_BOND * edge_bonds[c, i] + PULL_DENS * here[c], dz)
+        for c in range(3):
+            pull[c, 4] = totals[c]
 
     def slope_pulls(k, wanted):
         totals = [nothing(8, 128)] * 3
@@ -426,18 +473,19 @@
     slope[...] = nothing(6, 16, 128)
     slope_moved[...] = nothing(7, 6, 16, 128)
     loop(0, 6, take_tile)
-    pl.when(ahead & ~long_ahead)(far)
+    pl.when(ahead & least)(far)
     loop(0, 4, lambda k: move_tile(k, both_ways))
     move_tile(4, (-3, -2, -1))
     roll_slope(0, slope_value(0, ghost_density(0)))
 
     def own_whole(k):
-        totals = own_pairs(k, every, lambda dz: centre_of(k, dz))
+        totals = own_pairs(k)
         value = slope_value(k, totals[0])
         keep(k, totals, value)
         roll_slope(k, value)
 
     loop(1, 4, own_whole)
+    pl.when(ahead & ~least & ~most)(far)
     loop(1, 3, lambda k: move_slope(k, both_ways))
     move_slope(3, (-3, -2, -1))
     loop(1, 3, lambda k: add_pulls(k, slope_pulls(k, every)))
@@ -447,32 +495,23 @@
         for c in range(3):
             centres[c, i] = v[c]
 
-    def kept(dz):
-        return [centres[c, ZS.index(dz)] for c in range(3)]
-
-    part = own_pairs(4, behind, kept)
-    density[4] = part[0]
-    bond[4] = part[1]
-    for c in range(6):
-        pull[c + 4, 4] = part[2 + c]
-
-    pl.when(ahead & long_ahead)(far)
+    edge_pairs(behind, False)
+
+    pl.when(ahead & most)(far)
+    all_sent()
     far_got()
 
     for k in (6, 7):
         take_tile(k)
     move_tile(4, (1, 2, 3))
-    totals = own_pairs(4, beyond, kept)
-    totals = [totals[0] + density[4], totals[1] + bond[4]] + [totals[2 + c] + pull[c + 4, 4] for c in range(6)]
-    value = slope_value(4, totals[0])
-    keep(4, totals, value)
+    move_tile(5, both_ways)
+    value = slope_value(4, edge_pairs(beyond, True))
     roll_slope(4, value)
-    move_tile(5, both_ways)
     roll_slope(5, slope_value(5, ghost_density(5)))
+    move_slope(4, both_ways)
+    edge_pulls(value)
     move_slope(3, (1, 2, 3))
-    move_slope(4, both_ways)
     add_pulls(3, slope_pulls(3, beyond))
-    add_pulls(4, slope_pulls(4, every))
 
     first_part, back, back_rows, back_slots = back_indices()
 
@@ -495,7 +534,6 @@
         return BOND_SCALE * bond[k] - jnp.sqrt(d + 0.5) + 0.002 * d * d
 
     store(energy_ref, native(energy_of))
-    all_sent()
 
 
 def put_out(force_in, energy_in, force_ref, energy_ref, sems):
@@ -514,7 +552,6 @@
     return [
         f32(3, 8, 16, 128),
         pltpu.VMEM((4, 2, 128), jnp.int32),
-        f32(3, 8, 16, 128),
         f32(3, 4, 8, 16, 128),
         f32(3, 7, 6, 16, 128),
         f32(3, len(ZS), 8, 128),
@@ -523,7 +560,8 @@
         f32(7, 6, 16, 128),
         f32(6, 8, 128),
         f32(6, 8, 128),
-        f32(10, 6, 8, 128),
+        f32(3, 6, 8, 128),
+        f32(3, len(ZS), 8, 128),
         f32(3, len(VECTORS), 6, 8, 128),
         pltpu.SemaphoreType.DMA((2,)),
         pltpu.SemaphoreType.DMA((len(NEXT),)),

time: 22.5 us -> 22.4 us (level)
  no operation moved by 1% of the time
where the time goes in v4:
time: 22.4 us; the launch traced here: 22.2 us
  Pallas kernels  21.6 us (96%)
  between operations  0.64 us (3%)
    pallas_call x1, Pallas kernels, step(): pl.pallas_call(lambda *refs: atoms(sizes, *refs), out_shape=(pltpu.VMEM((...  20.9 us
    pallas_call x1, Pallas kernels, step(): pl.pallas_call(put_out, out_shape=[jax.ShapeDtypeStruct(x.shape, x.dtype)...  0.62 us

profile of v4, /device:TPU:1, one launch (start us, length us, event | category | flops | bytes accessed | tf_op | source)
XLA Modules:
  0.0 22.2 jit_solution(7298504767826625667)
XLA Ops:
  0.6 20.9 %shard_map.41 = (f32[3,4,1,2,128]{4,3,2,1,0:T(2,128)S(1)}, f32[4,1,2,128]{3,2,1,0:T(2,128)S(1)}) custom-call(f32[3,4,1,2,128]{4,3,2,1,0:T(2,128)} %refs_0_.1, s32[4,1,2,128]{3,2,1,0:T(2,128)} %refs_1_.1), custom_call_target="tpu_custom_call" | custom-call | tf_op jit(solution)/shard_map/pallas_call | solution.py:578
  21.6 0.6 %shard_map.42 = (f32[3,4,1,2,128]{4,3,2,1,0:T(2,128)}, f32[4,1,2,128]{3,2,1,0:T(2,128)}) custom-call(f32[3,4,1,2,128]{4,3,2,1,0:T(2,128)S(1)} %get-tuple-element.4.force_in, f32[4,1,2,128]{3,2,1,0:T(2,128)S(1)} %get-tuple-element.5.energy_in), custom_call_target="tpu_custom_call" | custom-call | tf_op jit(solution)/shard_map/pallas_call | solution.py:589

commit v5 on v4

--- a/solution.py
+++ b/solution.py
@@ -84,10 +84,9 @@
 
 
 YZ = sorted(((b, c) for b in (-1, 0, 1) for c in (-1, 0, 1)), key=lambda v: -abs(v[0]) - abs(v[1]))
-NEXT = [(a, b, c) for a in (0, 1, -1) for b, c in YZ if (a, b, c) != (0, 0, 0)]
-
-
-def exchange(sizes, raw_ref, send, recv, near_go):
+
+
+def exchange(sizes, raw_ref, counted, send, recv, near_go):
     n_x, n_y, n_z = sizes
     me_x, me_y, me_z = (lax.axis_index(a) for a in ("gx", "gy", "gz"))
     inner = (me_x == 1) | (me_x == 2)
@@ -143,41 +142,43 @@
         for b, c in around:
             when(there(b, c), lambda b=b, c=c: greet(my_outer, b, c))
 
-    def copy(v):
+    def copy(v, part):
         a, b, c = v
-        i = NEXT.index(v)
         x_from, x_to, x_n = {0: (2, 2, 4), 1: (4, 0, 2), -1: (2, 6, 2)}[a]
         z_from, z_to, z_n = {0: (1, 1, 2), 1: (2, 0, 1), -1: (1, 3, 1)}[c]
         row = 4 * (1 - b) + z_to
         return pltpu.make_async_remote_copy(
             src_ref=raw_ref.at[:, x_from : x_from + x_n, 4 + z_from : 4 + z_from + z_n],
             dst_ref=raw_ref.at[:, x_to : x_to + x_n, row : row + z_n],
-            send_sem=send.at[i],
-            recv_sem=recv.at[i],
+            send_sem=send.at[part],
+            recv_sem=recv.at[part],
             device_id=(me_x + a, me_y + b, me_z + c),
             device_id_type=MESH,
         )
 
-    def each(a, act, sign=1):
-        for b, c in YZ if sign == 1 else YZ[::-1]:
+    def start(a, part):
+        for b, c in YZ:
             if (a, b, c) != (0, 0, 0):
-                when(there(b, c, sign), lambda b=b, c=c: act(copy((a, b, c))))
-
-    start, sent, got = (lambda x: x.start()), (lambda x: x.wait_send()), (lambda x: x.wait_recv())
+                when(there(b, c), lambda b=b, c=c: copy((a, b, c), part).start())
+
     even = lax.rem(me_x, 2) == 0
-
-    def near_all(act, sign=1):
-        each(0, act, sign)
-        pl.when(even == (sign == 1))(lambda: each(1, act, sign))
-        pl.when(even == (sign != 1))(lambda: each(-1, act, sign))
-
-    def far_all(act, sign=1):
-        pl.when(me_x == (1 if sign == 1 else 2))(lambda: each(1, act, sign))
-        pl.when(me_x == (2 if sign == 1 else 1))(lambda: each(-1, act, sign))
+    end_y, end_z = (me_y == 0) | (me_y == n_y - 1), (me_z == 0) | (me_z == n_z - 1)
+
+    def wait(sem, each, less=0):
+        for last_y in (False, True):
+            for last_z in (False, True):
+                rows = each * (2 if last_y else 3) * (3 if last_z else 4) - less
+
+                def run(rows=rows):
+                    ref = counted.at[0:rows]
+                    pltpu.make_async_copy(ref, ref, sem).wait()
+
+                pl.when((end_y == last_y) & (end_z == last_z))(run)
 
     def far_inner():
         pl.semaphore_wait(barrier, count(YZ))
-        far_all(start)
+        pl.when(me_x == 1)(lambda: start(1, 1))
+        pl.when(me_x == 2)(lambda: start(-1, 1))
 
     def far():
         pl.when(inner)(far_inner)
@@ -189,17 +190,19 @@
     def near():
         pl.when(~inner)(near_outer)
         pl.when(inner)(lambda: pl.semaphore_wait(near_go, 1))
-        near_all(start)
+        start(0, 0)
+        pl.when(even)(lambda: start(1, 0))
+        pl.when(~even)(lambda: start(-1, 0))
 
     def near_got():
-        near_all(got, -1)
+        wait(recv.at[0], 18, 24)
 
     def far_got():
-        far_all(got, -1)
+        pl.when(inner)(lambda: wait(recv.at[1], 6))
 
     def all_sent():
-        near_all(sent)
-        far_all(sent)
+        wait(send.at[0], 18, 24)
+        pl.when(inner)(lambda: wait(send.at[1], 6))
 
     return enter, near, far, near_got, far_got, all_sent
 
@@ -225,10 +228,10 @@
     return sep, part * inside, near_in * inside * less, pull_bond, pull_dens
 
 
-def atoms(sizes, pos_ref, occ_ref, force_ref, energy_ref, raw, occ_v, rolled, moved, centres, slope, slope_rolled, slope_moved, density, bond, pull, edge_bonds, weighted, local, send, recv, near_go):
+def atoms(sizes, pos_ref, occ_ref, force_ref, energy_ref, raw, occ_v, rolled, moved, centres, slope, slope_rolled, slope_moved, density, bond, pull, edge_bonds, weighted, counted, local, send, recv, near_go):
     n_x, n_y, n_z = sizes
     me_x, me_y, me_z = (lax.axis_index(a) for a in ("gx", "gy", "gz"))
-    enter, near, far, near_got, far_got, all_sent = exchange(sizes, raw, send, recv, near_go)
+    enter, near, far, near_got, far_got, all_sent = exchange(sizes, raw, counted, send, recv, near_go)
     get_pos = pltpu.make_async_copy(pos_ref.at[:, :, 0], raw.at[:, 2:6, 5:7], local.at[0])
     get_occ = pltpu.make_async_copy(occ_ref.at[:, 0], occ_v, local.at[1])
     get_pos.start()
@@ -563,9 +566,10 @@
         f32(3, 6, 8, 128),
         f32(3, len(ZS), 8, 128),
         f32(3, len(VECTORS), 6, 8, 128),
+        f32(192, 128),
         pltpu.SemaphoreType.DMA((2,)),
-        pltpu.SemaphoreType.DMA((len(NEXT),)),
-        pltpu.SemaphoreType.DMA((len(NEXT),)),
+        pltpu.SemaphoreType.DMA((2,)),
+        pltpu.SemaphoreType.DMA((2,)),
         pltpu.SemaphoreType.REGULAR,
     ]
 

time: 22.4 us -> 21.9 us (0.978)
  Pallas kernels: 21.6 us -> 21.1 us
    pallas_call x1, Pallas kernels: 20.9 us -> 20.5 us  [step(): pl.pallas_call(lambda *refs: atoms(sizes, *refs), out_shape=(pltpu.VMEM((...]
where the time goes in v5:
time: 21.9 us; the launch traced here: 21.8 us
  Pallas kernels  21.1 us (96%)
  between operations  0.64 us (3%)
    pallas_call x1, Pallas kernels, step(): pl.pallas_call(lambda *refs: atoms(sizes, *refs), out_shape=(pltpu.VMEM((...  20.5 us
    pallas_call x1, Pallas kernels, step(): pl.pallas_call(put_out, out_shape=[jax.ShapeDtypeStruct(x.shape, x.dtype)...  0.62 us

profile of v5, /device:TPU:1, one launch (start us, length us, event | category | flops | bytes accessed | tf_op | source)
XLA Modules:
  0.0 21.8 jit_solution(13461798075336934880)
XLA Ops:
  0.6 20.5 %shard_map.41 = (f32[3,4,1,2,128]{4,3,2,1,0:T(2,128)S(1)}, f32[4,1,2,128]{3,2,1,0:T(2,128)S(1)}) custom-call(f32[3,4,1,2,128]{4,3,2,1,0:T(2,128)} %refs_0_.1, s32[4,1,2,128]{3,2,1,0:T(2,128)} %refs_1_.1), custom_call_target="tpu_custom_call" | custom-call | tf_op jit(solution)/shard_map/pallas_call | solution.py:582
  21.1 0.6 %shard_map.42 = (f32[3,4,1,2,128]{4,3,2,1,0:T(2,128)}, f32[4,1,2,128]{3,2,1,0:T(2,128)}) custom-call(f32[3,4,1,2,128]{4,3,2,1,0:T(2,128)S(1)} %get-tuple-element.4.force_in, f32[4,1,2,128]{3,2,1,0:T(2,128)S(1)} %get-tuple-element.5.energy_in), custom_call_target="tpu_custom_call" | custom-call | tf_op jit(solution)/shard_map/pallas_call | solution.py:593

commit v6 on v5

--- a/solution.py
+++ b/solution.py
@@ -86,7 +86,7 @@
 YZ = sorted(((b, c) for b in (-1, 0, 1) for c in (-1, 0, 1)), key=lambda v: -abs(v[0]) - abs(v[1]))
 
 
-def exchange(sizes, raw_ref, counted, send, recv, near_go):
+def exchange(sizes, pos_ref, occ_ref, raw_ref, far_occ, counted, send, recv, near_go):
     n_x, n_y, n_z = sizes
     me_x, me_y, me_z = (lax.axis_index(a) for a in ("gx", "gy", "gz"))
     inner = (me_x == 1) | (me_x == 2)
@@ -142,24 +142,40 @@
         for b, c in around:
             when(there(b, c), lambda b=b, c=c: greet(my_outer, b, c))
 
-    def copy(v, part):
+    def copies(v, part):
         a, b, c = v
-        x_from, x_to, x_n = {0: (2, 2, 4), 1: (4, 0, 2), -1: (2, 6, 2)}[a]
-        z_from, z_to, z_n = {0: (1, 1, 2), 1: (2, 0, 1), -1: (1, 3, 1)}[c]
+        x_from, x_to, x_n = {0: (0, 2, 4), 1: (2, 0, 2), -1: (0, 6, 2)}[a]
+        z_from, z_to, z_n = {0: (0, 1, 2), 1: (1, 0, 1), -1: (0, 3, 1)}[c]
         row = 4 * (1 - b) + z_to
-        return pltpu.make_async_remote_copy(
-            src_ref=raw_ref.at[:, x_from : x_from + x_n, 4 + z_from : 4 + z_from + z_n],
-            dst_ref=raw_ref.at[:, x_to : x_to + x_n, row : row + z_n],
-            send_sem=send.at[part],
-            recv_sem=recv.at[part],
-            device_id=(me_x + a, me_y + b, me_z + c),
-            device_id_type=MESH,
-        )
+
+        def remote(src, dst):
+            return pltpu.make_async_remote_copy(
+                src_ref=src,
+                dst_ref=dst,
+                send_sem=send.at[part],
+                recv_sem=recv.at[part],
+                device_id=(me_x + a, me_y + b, me_z + c),
+                device_id_type=MESH,
+            )
+
+        dst = raw_ref.at[:, x_to : x_to + x_n, row : row + z_n]
+        if part == 0:
+            return [remote(raw_ref.at[:, 2 + x_from : 2 + x_from + x_n, 5 + z_from : 5 + z_from + z_n], dst)]
+        at = (slice(x_from, x_from + x_n), 0, slice(z_from, z_from + z_n))
+        return [
+            remote(pos_ref.at[(slice(None), *at)], dst),
+            remote(occ_ref.at[at], far_occ.at[:, row : row + z_n]),
+        ]
 
     def start(a, part):
         for b, c in YZ:
             if (a, b, c) != (0, 0, 0):
-                when(there(b, c), lambda b=b, c=c: copy((a, b, c), part).start())
+
+                def run(v=(a, b, c)):
+                    for x in copies(v, part):
+                        x.start()
+
+                when(there(b, c), run)
 
     even = lax.rem(me_x, 2) == 0
     end_y, end_z = (me_y == 0) | (me_y == n_y - 1), (me_z == 0) | (me_z == n_z - 1)
@@ -198,11 +214,11 @@
         wait(recv.at[0], 18, 24)
 
     def far_got():
-        pl.when(inner)(lambda: wait(recv.at[1], 6))
+        pl.when(inner)(lambda: wait(recv.at[1], 8))
 
     def all_sent():
         wait(send.at[0], 18, 24)
-        pl.when(inner)(lambda: wait(send.at[1], 6))
+        pl.when(inner)(lambda: wait(send.at[1], 8))
 
     return enter, near, far, near_got, far_got, all_sent
 
@@ -228,12 +244,13 @@
     return sep, part * inside, near_in * inside * less, pull_bond, pull_dens
 
 
-def atoms(sizes, pos_ref, occ_ref, force_ref, energy_ref, raw, occ_v, rolled, moved, centres, slope, slope_rolled, slope_moved, density, bond, pull, edge_bonds, weighted, counted, local, send, recv, near_go):
+def atoms(sizes, pos_ref, occ_ref, force_ref, energy_ref, raw, occ_v, far_occ, rolled, moved, centres, slope, slope_rolled, slope_moved, density, bond, pull, edge_bonds, weighted, counted, local, send, recv, near_go):
     n_x, n_y, n_z = sizes
     me_x, me_y, me_z = (lax.axis_index(a) for a in ("gx", "gy", "gz"))
-    enter, near, far, near_got, far_got, all_sent = exchange(sizes, raw, counted, send, recv, near_go)
+    enter, near, far, near_got, far_got, all_sent = exchange(sizes, pos_ref, occ_ref, raw, far_occ, counted, send, recv, near_go)
     get_pos = pltpu.make_async_copy(pos_ref.at[:, :, 0], raw.at[:, 2:6, 5:7], local.at[0])
     get_occ = pltpu.make_async_copy(occ_ref.at[:, 0], occ_v, local.at[1])
+    far_occ[...] = jnp.ones((2, 16, 128), jnp.int32)
     get_pos.start()
     get_occ.start()
 
@@ -250,8 +267,8 @@
     at_once = (me_x == 2) & most
 
     def send_first():
+        far()
         load()
-        far()
         enter()
 
     def greet_first():
@@ -304,7 +321,7 @@
 
     near_got()
 
-    def take_tile(k):
+    def take_tile(k, occupied=None):
         t = place(k, 8)
         out_x = ((me_x == 0) & (t < 2)) | ((me_x == n_x - 1) & (t > 5))
         far_x = jnp.where(out_x, far_away, 0.0) + (t - 2).astype(jnp.float32) * TILE_X
@@ -318,7 +335,10 @@
                 shift_z,
             ]
             for c in range(3):
-                v = pick(pick(raw[c, t, rows], turn[0], 1), turn[1], 0)
+                v = raw[c, t, rows]
+                if c == 0 and occupied is not None:
+                    v = v + jnp.where(occupied[rows] != 0, 0.0, far_away)
+                v = pick(pick(v, turn[0], 1), turn[1], 0)
                 for a in range(4):
                     rolled[c, a, k, rows] = (pick(v, planes[a], 1) + shifts[c]) * unit
 
@@ -505,7 +525,7 @@
     far_got()
 
     for k in (6, 7):
-        take_tile(k)
+        take_tile(k, far_occ.at[jnp.where(ahead, k - 6, 7 - k)])
     move_tile(4, (1, 2, 3))
     move_tile(5, both_ways)
     value = slope_value(4, edge_pairs(beyond, True))
@@ -555,6 +575,7 @@
     return [
         f32(3, 8, 16, 128),
         pltpu.VMEM((4, 2, 128), jnp.int32),
+        pltpu.VMEM((2, 16, 128), jnp.int32),
         f32(3, 4, 8, 16, 128),
         f32(3, 7, 6, 16, 128),
         f32(3, len(ZS), 8, 128),

time: 21.9 us -> 21.8 us (level)
  no operation moved by 1% of the time
where the time goes in v6:
time: 21.8 us; the launch traced here: 21.7 us
  Pallas kernels  21 us (96%)
  between operations  0.64 us (3%)
    pallas_call x1, Pallas kernels, step(): pl.pallas_call(lambda *refs: atoms(sizes, *refs), out_shape=(pltpu.VMEM((...  20.4 us
    pallas_call x1, Pallas kernels, step(): pl.pallas_call(put_out, out_shape=[jax.ShapeDtypeStruct(x.shape, x.dtype)...  0.62 us

profile of v6, /device:TPU:1, one launch (start us, length us, event | category | flops | bytes accessed | tf_op | source)
XLA Modules:
  0.0 21.7 jit_solution(3286280237648423833)
XLA Ops:
  0.6 20.4 %shard_map.41 = (f32[3,4,1,2,128]{4,3,2,1,0:T(2,128)S(1)}, f32[4,1,2,128]{3,2,1,0:T(2,128)S(1)}) custom-call(f32[3,4,1,2,128]{4,3,2,1,0:T(2,128)} %refs_0_.1, s32[4,1,2,128]{3,2,1,0:T(2,128)} %refs_1_.1), custom_call_target="tpu_custom_call" | custom-call | tf_op jit(solution)/shard_map/pallas_call | solution.py:603
  21.0 0.6 %shard_map.42 = (f32[3,4,1,2,128]{4,3,2,1,0:T(2,128)}, f32[4,1,2,128]{3,2,1,0:T(2,128)}) custom-call(f32[3,4,1,2,128]{4,3,2,1,0:T(2,128)S(1)} %get-tuple-element.4.force_in, f32[4,1,2,128]{3,2,1,0:T(2,128)S(1)} %get-tuple-element.5.energy_in), custom_call_target="tpu_custom_call" | custom-call | tf_op jit(solution)/shard_map/pallas_call | solution.py:614

commit v7 on v6

--- a/solution.py
+++ b/solution.py
@@ -216,11 +216,13 @@
     def far_got():
         pl.when(inner)(lambda: wait(recv.at[1], 8))
 
-    def all_sent():
+    def near_sent():
         wait(send.at[0], 18, 24)
+
+    def far_sent():
         pl.when(inner)(lambda: wait(send.at[1], 8))
 
-    return enter, near, far, near_got, far_got, all_sent
+    return enter, near, far, near_got, far_got, near_sent, far_sent
 
 
 def pair_density(centre, near):
@@ -247,7 +249,7 @@
 def atoms(sizes, pos_ref, occ_ref, force_ref, energy_ref, raw, occ_v, far_occ, rolled, moved, centres, slope, slope_rolled, slope_moved, density, bond, pull, edge_bonds, weighted, counted, local, send, recv, near_go):
     n_x, n_y, n_z = sizes
     me_x, me_y, me_z = (lax.axis_index(a) for a in ("gx", "gy", "gz"))
-    enter, near, far, near_got, far_got, all_sent = exchange(sizes, pos_ref, occ_ref, raw, far_occ, counted, send, recv, near_go)
+    enter, near, far, near_got, far_got, near_sent, far_sent = exchange(sizes, pos_ref, occ_ref, raw, far_occ, counted, send, recv, near_go)
     get_pos = pltpu.make_async_copy(pos_ref.at[:, :, 0], raw.at[:, 2:6, 5:7], local.at[0])
     get_occ = pltpu.make_async_copy(occ_ref.at[:, 0], occ_v, local.at[1])
     far_occ[...] = jnp.ones((2, 16, 128), jnp.int32)
@@ -268,8 +270,8 @@
 
     def send_first():
         far()
+        enter()
         load()
-        enter()
 
     def greet_first():
         enter()
@@ -520,8 +522,8 @@
 
     edge_pairs(behind, False)
 
+    near_sent()
     pl.when(ahead & most)(far)
-    all_sent()
     far_got()
 
     for k in (6, 7):
@@ -557,6 +559,7 @@
         return BOND_SCALE * bond[k] - jnp.sqrt(d + 0.5) + 0.002 * d * d
 
     store(energy_ref, native(energy_of))
+    far_sent()
 
 
 def put_out(force_in, energy_in, force_ref, energy_ref, sems):

time: 21.8 us -> 21.6 us (level)
    pallas_call x1, Pallas kernels: 20.4 us -> 20.1 us  [step(): pl.pallas_call(lambda *refs: atoms(sizes, *refs), out_shape=(pltpu.VMEM((...]
where the time goes in v7:
time: 21.6 us; the launch traced here: 21.4 us
  Pallas kernels  20.8 us (96%)
  between operations  0.64 us (3%)
    pallas_call x1, Pallas kernels, step(): pl.pallas_call(lambda *refs: atoms(sizes, *refs), out_shape=(pltpu.VMEM((...  20.1 us
    pallas_call x1, Pallas kernels, step(): pl.pallas_call(put_out, out_shape=[jax.ShapeDtypeStruct(x.shape, x.dtype)...  0.62 us

profile of v7, /device:TPU:1, one launch (start us, length us, event | category | flops | bytes accessed | tf_op | source)
XLA Modules:
  0.0 21.4 jit_solution(8385538210925107123)
XLA Ops:
  0.6 20.1 %shard_map.41 = (f32[3,4,1,2,128]{4,3,2,1,0:T(2,128)S(1)}, f32[4,1,2,128]{3,2,1,0:T(2,128)S(1)}) custom-call(f32[3,4,1,2,128]{4,3,2,1,0:T(2,128)} %refs_0_.1, s32[4,1,2,128]{3,2,1,0:T(2,128)} %refs_1_.1), custom_call_target="tpu_custom_call" | custom-call | tf_op jit(solution)/shard_map/pallas_call | solution.py:606
  20.8 0.6 %shard_map.42 = (f32[3,4,1,2,128]{4,3,2,1,0:T(2,128)}, f32[4,1,2,128]{3,2,1,0:T(2,128)}) custom-call(f32[3,4,1,2,128]{4,3,2,1,0:T(2,128)S(1)} %get-tuple-element.4.force_in, f32[4,1,2,128]{3,2,1,0:T(2,128)S(1)} %get-tuple-element.5.energy_in), custom_call_target="tpu_custom_call" | custom-call | tf_op jit(solution)/shard_map/pallas_call | solution.py:617
